TPU v7x, 256 devices: a whole 4x4x8 slice. The times are simulated.
256 devices in a mesh: energy: 16 (over x, z_lo), tile: 16 (over z_hi, y, core).
Axes of the slice: x: 4, y: 4, z: 8 (z_hi: 2, z_lo: 4; z = z_hi * 4 + z_lo), core: 2. Of those that a mesh axis runs over, the one named last changes fastest.
Arguments:
- object_tiles: float32 [16, 2, 16, 512, 512], P('energy', None, 'tile'), may hold values from -6 to 6
- probe_wave: float32 [16, 2, 256, 256], P('energy'), may hold values from -6 to 6
- measured: bfloat16 [16, 16, 16, 256, 256], P('energy', 'tile'), may hold values from 0 to 2
- positions: int32 [16, 16, 2], P('tile'), may hold values from 0 to 511, as said below
- materials: float32 [2, 16, 8], replicated, may hold values from -6 to 6
Outputs:
- fitted: float32 [16, 2, 16, 512, 512], P('energy', None, 'tile')
Inputs may be any that keep to these rules, and one draw needn't show every extreme that they name: `positions`: each entry is the corner of a 256 x 256 patch, given inside its tile; in every tile some patch has row corner 512 - 1 and some has column corner 512 - 1.
All inputs are finite; a program needn't handle non-finite values.
Results may differ from a plain program's by a relative error of at most 0.0013.
Values sent between devices are 32-bit elements; how exact they have to be, the bound alone decides.
No kernel may reach another device: no remote copies, remote signals or barrier semaphores. Data moves between devices by JAX's collectives and lax.ppermute only.
A program may use at most 64 MiB of HBM per device.

v0:
```python
import math

import jax
import jax.numpy as jnp
from jax import lax
from jax.sharding import PartitionSpec as P

TILE_COLS = 4
FIT_STEPS = 10


amplitude_floor = 0.5


def shifted(value, axis, steps):
    count = lax.axis_size(axis)
    pairs = [(source, (source + steps) % count) for source in range(count)]
    return lax.ppermute(value, axis, pairs)


def fourier_tables(length, direction):
    counter = jnp.arange(length, dtype=jnp.int32)
    products = counter[:, None] * counter[None, :] % length
    angles = 2.0 * math.pi / length * products.astype(jnp.float32)
    cosine = jnp.cos(angles)
    sine = direction * jnp.sin(angles)
    left_table = jnp.concatenate(
        [jnp.concatenate([cosine, sine], 1), jnp.concatenate([-sine, cosine], 1)], 0
    ).astype(jnp.bfloat16)
    right_table = jnp.concatenate(
        [jnp.concatenate([cosine, -sine], 1), jnp.concatenate([sine, cosine], 1)], 0
    ).astype(jnp.bfloat16)
    return (left_table, right_table)


def transform(real_part, imag_part, left_table, right_table):
    length = real_part.shape[0]
    stacked = jnp.concatenate([real_part, imag_part], 0).astype(jnp.bfloat16)
    inner = jnp.dot(left_table, stacked, preferred_element_type=jnp.float32)
    beside = jnp.concatenate([inner[:length], inner[length:]], 1).astype(jnp.bfloat16)
    outer = jnp.dot(beside, right_table, preferred_element_type=jnp.float32) / length
    return (outer[:, :length], outer[:, length:])


def patch_gradient(
    field_real, field_imag, probe_real, probe_imag, amplitude, row_start, col_start, tables
):
    length = probe_real.shape[0]
    piece_real = lax.dynamic_slice(field_real, (row_start, col_start), (length, length))
    piece_imag = lax.dynamic_slice(field_imag, (row_start, col_start), (length, length))
    exit_real = probe_real * piece_real - probe_imag * piece_imag
    exit_imag = probe_real * piece_imag + probe_imag * piece_real
    far_real, far_imag = transform(exit_real, exit_imag, tables[0], tables[1])
    magnitude = jnp.sqrt(far_real * far_real + far_imag * far_imag)
    factor = amplitude.astype(jnp.float32) / jnp.maximum(magnitude, amplitude_floor) - 1.0
    back_real, back_imag = transform(factor * far_real, factor * far_imag, tables[2], tables[3])
    return (
        probe_real * back_real + probe_imag * back_imag,
        probe_real * back_imag - probe_imag * back_real,
    )


def fit_materials(data, materials):
    high = lax.Precision.HIGHEST
    gram = jnp.einsum("rem,ren->mn", materials, materials, precision=high)
    rate = 1.0 / jnp.trace(gram)
    target = jnp.einsum("rem,rep->mp", materials, data, precision=high)

    def descend(number, coefficients):
        slope = jnp.dot(gram, coefficients, precision=high) - target
        return jnp.maximum(coefficients - rate * slope, 0.0)

    return lax.fori_loop(0, FIT_STEPS, descend, jnp.zeros_like(target))


def fitted_spectra(materials, coefficients):
    return jnp.einsum("rem,mp->rep", materials, coefficients, precision=lax.Precision.HIGHEST)


def body(object_tiles, probe_wave, measured, positions, materials):
    own_object = object_tiles[0, :, 0]
    tile_px = own_object.shape[-1]
    length = probe_wave.shape[-1]
    count = measured.shape[2]
    tile_count = lax.axis_size("tile")
    row_step = TILE_COLS % tile_count
    right_strip = shifted(own_object[:, :, :length], "tile", -1)
    widened = jnp.concatenate([own_object, right_strip], 2)
    lower_strip = shifted(widened[:, :length, :], "tile", -row_step)
    extended = jnp.concatenate([widened, lower_strip], 1)
    forward = fourier_tables(length, 1.0)
    inverse = fourier_tables(length, -1.0)
    tables = (forward[0], forward[1], inverse[0], inverse[1])
    probe_real = probe_wave[0, 0]
    probe_imag = probe_wave[0, 1]
    own_measured = measured[0, 0]
    corners = positions[0]
    anchor = jnp.zeros((), jnp.int32)

    def accumulate(number, gradient):
        row_start = corners[number, 0]
        col_start = corners[number, 1]
        term_real, term_imag = patch_gradient(
            extended[0],
            extended[1],
            probe_real,
            probe_imag,
            own_measured[number],
            row_start,
            col_start,
            tables,
        )
        current = lax.dynamic_slice(gradient, (anchor, row_start, col_start), (2, length, length))
        return lax.dynamic_update_slice(
            gradient, current + jnp.stack([term_real, term_imag]), (anchor, row_start, col_start)
        )

    gradient = lax.fori_loop(0, count, accumulate, jnp.zeros_like(extended))
    from_above = shifted(gradient[:, tile_px:, :], "tile", row_step)
    upper = jnp.concatenate(
        [gradient[:, :length, :] + from_above, gradient[:, length:tile_px, :]], 1
    )
    from_left = shifted(upper[:, :, tile_px:], "tile", 1)
    summed = jnp.concatenate([upper[:, :, :length] + from_left, upper[:, :, length:tile_px]], 2)
    peak = jnp.max(probe_real * probe_real + probe_imag * probe_imag)
    updated = own_object + summed / peak
    groups = lax.axis_size("energy")
    pixels = tile_px * tile_px
    group_width = pixels // groups
    outgoing = updated.reshape(2, 1, groups, group_width)
    arrived = lax.all_to_all(outgoing, "energy", split_axis=2, concat_axis=1, tiled=True)
    coefficients = fit_materials(arrived.reshape(2, groups, group_width), materials)
    spectra = fitted_spectra(materials, coefficients).reshape(2, groups, 1, group_width)
    returned = lax.all_to_all(spectra, "energy", split_axis=1, concat_axis=2, tiled=True)
    result = returned.reshape(2, tile_px, tile_px)
    return result.reshape(1, 2, 1, tile_px, tile_px)


def solution(mesh):
    in_specs = (
        P("energy", None, "tile", None, None),
        P("energy", None, None, None),
        P("energy", "tile", None, None, None),
        P("tile", None, None),
        P(),
    )
    out_specs = P("energy", None, "tile", None, None)
    return jax.shard_map(body, mesh=mesh, in_specs=in_specs, out_specs=out_specs, check_vma=False)
```

profile of v0, /device:TPU:9, one launch (start us, length us, event | category | flops | bytes accessed | tf_op | source)
XLA Modules:
  0.0 671.4 jit_solution(6523664478855284221)
XLA Ops:
  2.2 13.7 %collective-permute-done = f32[2,512,256]{2,1,0:T(8,128)S(1)} collective-permute-done((f32[2,512,256]{2,1,0:T(8,128)S(1)}, f32[2,512,256]{2,1,0:T(8,128)S(1)}, u32[]{:S(2)}, u32[]{:S(2)}) %collective-permute-start) | collective-permute-done | bytes 1048608 | tf_op jit(solution)/shard_map/ppermute | solution.py:18
  17.4 23.7 %collective-permute-start.1 = (f32[2,256,768]{2,1,0:T(8,128)}, f32[2,256,768]{2,1,0:T(8,128)}, u32[]{:S(2)}, u32[]{:S(2)}) collective-permute-start(f32[2,256,768]{2,1,0:T(8,128)} %pad_maximum_fusion.1), channel_id=1, source_target_pairs={{0,12},{1,13},{2,14},{3,15},{4,0},{5,1},{6,2},{7,3},{8,4},{9,5},{1... | collective-permute-start | bytes 4718600 | tf_op jit(solution)/shard_map/ppermute | solution.py:18
  45.7 48.1 %collective-permute-done.1 = f32[2,256,768]{2,1,0:T(8,128)} collective-permute-done((f32[2,256,768]{2,1,0:T(8,128)}, f32[2,256,768]{2,1,0:T(8,128)}, u32[]{:S(2)}, u32[]{:S(2)}) %collective-permute-start.1) | collective-permute-done | bytes 1572896 | tf_op jit(solution)/shard_map/ppermute | solution.py:18
  93.7 4.0 pad_maximum_fusion
  100.2 352.7 %while.26 = (s32[]{:T(128)}, f32[2,768,768]{2,1,0:T(8,128)}, s32[16,2]{0,1:T(2,128)S(1)}, bf16[16,256,256]{2,1,0:T(8,128)(2,1)}, f32[2,768,768]{2,1,0:T(8,128)},...) while((s32[]{:T(128)}, f32[2,768,768]{2,1,0:T(8,128)}, ...), condition=%wide.region_1.2_spmd, body=%wide.region_0.1_spmd.sunk | while | flops 541392896 | bytes 21627124 | solution.py:118
  115.7 6.5 dynamic_update_slice.11
  126.6 2.7 fusion.87
  137.7 6.0 dynamic_update_slice.11
  148.1 2.7 fusion.87
  159.2 6.8 %dynamic_update_slice.11 = f32[2,768,768]{2,1,0:T(8,128)} dynamic-update-slice(f32[2,768,768]{2,1,0:T(8,128)} %get-tuple-element.519, f32[2,256,256]{2,1,0:T(8,128)S(1)} %maximum_add_fusion.2, s32[]{:T(128)} %constant.115.clone.1..sunk, s32[]{:T(128)S(6)} %select_n.102, s32[]{:T(128)S(6)} %select_n.103) | dynamic-update-slice | bytes 1048580 | tf_op jit(solution)/shard_map/while/body/eval_jaxpr/dynamic_update_slice | solution.py:114
  181.5 6.2 dynamic_update_slice.11
  203.2 6.2 dynamic_update_slice.11
  224.9 6.6 dynamic_update_slice.11
  247.0 6.8 %dynamic_update_slice.11 = f32[2,768,768]{2,1,0:T(8,128)} dynamic-update-slice(f32[2,768,768]{2,1,0:T(8,128)} %get-tuple-element.519, f32[2,256,256]{2,1,0:T(8,128)S(1)} %maximum_add_fusion.2, s32[]{:T(128)} %constant.115.clone.1..sunk, s32[]{:T(128)S(6)} %select_n.102, s32[]{:T(128)S(6)} %select_n.103) | dynamic-update-slice | bytes 1048580 | tf_op jit(solution)/shard_map/while/body/eval_jaxpr/dynamic_update_slice | solution.py:114
  269.4 6.5 dynamic_update_slice.11
  291.4 6.7 %dynamic_update_slice.11 = f32[2,768,768]{2,1,0:T(8,128)} dynamic-update-slice(f32[2,768,768]{2,1,0:T(8,128)} %get-tuple-element.519, f32[2,256,256]{2,1,0:T(8,128)S(1)} %maximum_add_fusion.2, s32[]{:T(128)} %constant.115.clone.1..sunk, s32[]{:T(128)S(6)} %select_n.102, s32[]{:T(128)S(6)} %select_n.103) | dynamic-update-slice | bytes 1048580 | tf_op jit(solution)/shard_map/while/body/eval_jaxpr/dynamic_update_slice | solution.py:114
  313.6 6.8 %dynamic_update_slice.11 = f32[2,768,768]{2,1,0:T(8,128)} dynamic-update-slice(f32[2,768,768]{2,1,0:T(8,128)} %get-tuple-element.519, f32[2,256,256]{2,1,0:T(8,128)S(1)} %maximum_add_fusion.2, s32[]{:T(128)} %constant.115.clone.1..sunk, s32[]{:T(128)S(6)} %select_n.102, s32[]{:T(128)S(6)} %select_n.103) | dynamic-update-slice | bytes 1048580 | tf_op jit(solution)/shard_map/while/body/eval_jaxpr/dynamic_update_slice | solution.py:114
  335.9 6.2 dynamic_update_slice.11
  357.6 6.5 dynamic_update_slice.11
  379.6 6.5 dynamic_update_slice.11
  401.7 6.8 %dynamic_update_slice.11 = f32[2,768,768]{2,1,0:T(8,128)} dynamic-update-slice(f32[2,768,768]{2,1,0:T(8,128)} %get-tuple-element.519, f32[2,256,256]{2,1,0:T(8,128)S(1)} %maximum_add_fusion.2, s32[]{:T(128)} %constant.115.clone.1..sunk, s32[]{:T(128)S(6)} %select_n.102, s32[]{:T(128)S(6)} %select_n.103) | dynamic-update-slice | bytes 1048580 | tf_op jit(solution)/shard_map/while/body/eval_jaxpr/dynamic_update_slice | solution.py:114
  424.0 6.9 %dynamic_update_slice.11 = f32[2,768,768]{2,1,0:T(8,128)} dynamic-update-slice(f32[2,768,768]{2,1,0:T(8,128)} %get-tuple-element.519, f32[2,256,256]{2,1,0:T(8,128)S(1)} %maximum_add_fusion.2, s32[]{:T(128)} %constant.115.clone.1..sunk, s32[]{:T(128)S(6)} %select_n.102, s32[]{:T(128)S(6)} %select_n.103) | dynamic-update-slice | bytes 1048580 | tf_op jit(solution)/shard_map/while/body/eval_jaxpr/dynamic_update_slice | solution.py:114
  446.3 6.6 dynamic_update_slice.11
  454.5 65.5 %collective-permute-done.2 = f32[2,256,768]{2,1,0:T(8,128)S(1)} collective-permute-done((f32[2,256,768]{2,1,0:T(8,128)S(1)}, f32[2,256,768]{2,1,0:T(8,128)S(1)}, u32[]{:S(2)}, u32[]{:S(2)}) %collective-permute-start.2) | collective-permute-done | bytes 1572896 | tf_op jit(solution)/shard_map/ppermute | solution.py:18
  526.4 9.9 %collective-permute-done.3 = f32[2,512,256]{2,1,0:T(8,128)} collective-permute-done((f32[2,512,256]{2,1,0:T(8,128)}, f32[2,512,256]{2,1,0:T(8,128)}, u32[]{:S(2)}, u32[]{:S(2)}) %collective-permute-start.3) | collective-permute-done | bytes 1048608 | tf_op jit(solution)/shard_map/ppermute | solution.py:18
  540.2 2.9 div.42
  545.0 2.9 copy.8
  548.0 4.4 all-to-all-start
  553.8 48.4 %all-to-all-done = f32[2,1,16,16384]{3,0,1,2:T(2,128)} async-done(((f32[2,1,16,16384]{3,0,1,2:T(2,128)}), f32[2,1,16,16384]{3,0,1,2:T(2,128)}, u32[]{:S(2)}, u32[]{:S(2)}) %all-to-all-start) | async-done | bytes 2097184 | tf_op jit(solution)/shard_map/all_to_all | solution.py:131
  602.2 3.9 convolution_bitcast_fusion.1
  606.1 7.1 %while.27 = (s32[]{:T(128)}, f32[8,16384]{1,0:T(8,128)S(1)}, f32[]{:T(128)}, f32[8,8]{1,0:T(8,128)S(1)}, f32[8,16384]{1,0:T(8,128)S(1)}, /*index=5*/s32[]{:T(128)}, s32[]{:T(128)}) while((s32[]{:T(128)}, f32[8,16384]{1,0:T(8,128)S(1)}, f32[]{:T(128)}, f32[8,8]{1,0:T(8,128)S(1)}, f32[8,16384]{1,0:T(8,128)S(1)}, ...), condition=%wide.region_5.6_spmd.clone, body=%wide.region_4.5_spmd.clone.sunk | while | flops 13369347 | bytes 2621787 | solution.py:73
  616.6 52.0 %all_to_all.8 = f32[2,16,1,16384]{3,0,2,1:T(2,128)S(1)} all-to-all(f32[2,16,1,16384]{3,0,2,1:T(2,128)S(1)} %copy.10), channel_id=1, replica_groups=mesh['energy'=16,'tile'=16] {'energy'}, dimensions={1} | all-to-all | bytes 4194304 | tf_op jit(solution)/shard_map/all_to_all | solution.py:134
  (259 shorter events, 218.2 us)
Async XLA Ops:
  0.0 552.4 %copy-start = (f32[2,16,8]{1,2,0:T(8,128)S(1)}, f32[2,16,8]{1,2,0:T(8,128)}, u32[]{:S(2)}) copy-start(f32[2,16,8]{1,2,0:T(8,128)} %param.13) | copy-start | bytes 3076
  0.0 15.9 %copy-start.1 = (f32[1,2,1,512,512]{4,3,2,1,0:T(8,128)S(1)}, f32[1,2,1,512,512]{4,3,2,1,0:T(8,128)}, u32[]{:S(2)}) copy-start(f32[1,2,1,512,512]{4,3,2,1,0:T(8,128)} %param.9) | copy-start | bytes 6291460
  1.5 14.4 %collective-permute-start = (f32[2,512,256]{2,1,0:T(8,128)S(1)}, f32[2,512,256]{2,1,0:T(8,128)S(1)}, u32[]{:S(2)}, u32[]{:S(2)}) collective-permute-start(f32[2,512,256]{2,1,0:T(8,128)S(1)} %slice.152), channel_id=1, source_target_pairs={{0,15},{1,0},{2,1},{3,2},{4,3},{5,4},{6,5},{7,6},{8,7},{9,8},{10,9... | collective-permute-start | bytes 3145736 | tf_op jit(solution)/shard_map/ppermute | solution.py:18
  15.9 1.5 copy-start.7
  17.4 28.2 %copy-start.9 = (f32[1,2,256,256]{3,2,1,0:T(8,128)S(1)}, f32[1,2,256,256]{3,2,1,0:T(8,128)}, u32[]{:S(2)}) copy-start(f32[1,2,256,256]{3,2,1,0:T(8,128)} %param.10) | copy-start | bytes 1572868
  17.4 76.4 %collective-permute-start.1 = (f32[2,256,768]{2,1,0:T(8,128)}, f32[2,256,768]{2,1,0:T(8,128)}, u32[]{:S(2)}, u32[]{:S(2)}) collective-permute-start(f32[2,256,768]{2,1,0:T(8,128)} %pad_maximum_fusion.1), channel_id=1, source_target_pairs={{0,12},{1,13},{2,14},{3,15},{4,0},{5,1},{6,2},{7,3},{8,4},{9,5},{1... | collective-permute-start | bytes 4718600 | tf_op jit(solution)/shard_map/ppermute | solution.py:18
  43.0 50.7 %copy-start.8 = (f32[2,512,256]{2,1,0:T(8,128)S(1)}, f32[2,512,256]{2,1,0:T(8,128)}, u32[]{:S(2)}) copy-start(f32[2,512,256]{2,1,0:T(8,128)} %copy-done.7) | copy-start | bytes 3145732
  97.7 2.5 copy-start.11
  454.4 65.6 %collective-permute-start.2 = (f32[2,256,768]{2,1,0:T(8,128)S(1)}, f32[2,256,768]{2,1,0:T(8,128)S(1)}, u32[]{:S(2)}, u32[]{:S(2)}) collective-permute-start(f32[2,256,768]{2,1,0:T(8,128)S(1)} %slice.139), channel_id=1, source_target_pairs={{0,4},{1,5},{2,6},{3,7},{4,8},{5,9},{6,10},{7,11},{8,12},{9,13},{1... | collective-permute-start | bytes 4718600 | tf_op jit(solution)/shard_map/ppermute | solution.py:18
  522.2 1.5 copy-start.2
  522.3 2.0 copy-start.4
  524.2 1.5 copy-start.10
  524.2 12.1 %collective-permute-start.3 = (f32[2,512,256]{2,1,0:T(8,128)}, f32[2,512,256]{2,1,0:T(8,128)}, u32[]{:S(2)}, u32[]{:S(2)}) collective-permute-start(f32[2,512,256]{2,1,0:T(8,128)} %fusion.34), channel_id=1, source_target_pairs={{0,1},{1,2},{2,3},{3,4},{4,5},{5,6},{6,7},{7,8},{8,9},{9,10},{10,1... | collective-permute-start | bytes 3145736 | tf_op jit(solution)/shard_map/ppermute | solution.py:18
  526.4 11.5 %copy-start.3 = (f32[2,256,768]{2,1,0:T(8,128)S(1)}, f32[2,256,768]{2,1,0:T(8,128)}, u32[]{:S(2)}) copy-start(f32[2,256,768]{2,1,0:T(8,128)} %copy-done.2) | copy-start | bytes 4718596
  526.4 11.5 %copy-start.5 = (f32[2,256,768]{2,1,0:T(8,128)S(1)}, f32[2,256,768]{2,1,0:T(8,128)}, u32[]{:S(2)}) copy-start(f32[2,256,768]{2,1,0:T(8,128)} %copy-done.4) | copy-start | bytes 4718596
  540.2 2.9 copy-start.6
  548.0 54.2 %all-to-all-start = ((f32[2,1,16,16384]{3,0,1,2:T(2,128)}), f32[2,1,16,16384]{3,0,1,2:T(2,128)}, u32[]{:S(2)}, u32[]{:S(2)}) async-start(f32[2,1,16,16384]{3,0,1,2:T(2,128)} %copy.8), calls=%async_computation | async-start | bytes 4194304 | tf_op jit(solution)/shard_map/all_to_all | solution.py:131
where the time goes:
time: 681 us; the launch traced here: 671 us
  waiting for transfers between devices  186 us (27%)
  local copies, waits for them, and re-layouts  177 us (26%)
  matrix products  101 us (15%)
  other arithmetic  63.7 us (9%)
  loops' own time  63 us (9%)
  blocking collectives  52 us (8%)
  starting transfers between devices  29 us (4%)
    ppermute x4, waiting for transfers between devices, shifted(): return lax.ppermute(value, axis, pairs)  137 us
    dynamic_update_slice x16, local copies, waits for them, and re-layouts, accumulate(): lax.dynamic_update_slice(gradient, current + jnp.stack([term_real, term_i...  105 us
    another operation x1, loops' own time, body(): gradient = lax.fori_loop(0, count, accumulate, jnp.zeros_like(extended))  62.6 us
    all_to_all x1, blocking collectives, body(): lax.all_to_all(spectra, 'energy', split_axis=1, concat_axis=2, tiled=True)  52 us
    all_to_all x1, waiting for transfers between devices, body(): lax.all_to_all(outgoing, 'energy', split_axis=2, concat_axis=1, tiled=True)  48.4 us
    dot_general x32, matrix products, transform(): inner = jnp.dot(left_table, stacked, preferred_element_type=jnp.float32)  44.5 us
    dot_general x32, matrix products, transform(): jnp.dot(beside, right_table, preferred_element_type=jnp.float32) / length  43.5 us
    slice x16, local copies, waits for them, and re-layouts, accumulate(): extended[0]  42.9 us
  transfers between devices with their start and end apart: 5, of which 5 were waited for; matrix products, arithmetic and copies ran while one was open for 1% of the time, Pallas kernels for 0%

commit v1 on v0

v1 whole, which is shorter than its diff:
```python
import functools

import jax
import jax.numpy as jnp
import ml_dtypes
import numpy as np
from jax import lax
from jax.experimental import pallas as pl
from jax.experimental.pallas import tpu as pltpu
from jax.sharding import PartitionSpec as P

TILE_COLS = 4
FIT_STEPS = 10
AMPLITUDE_FLOOR = 0.5
LANES = 128
VMEM_BYTES = 48 * 2**20


def shifted(value, axis, steps):
    count = lax.axis_size(axis)
    pairs = [(source, (source + steps) % count) for source in range(count)]
    return lax.ppermute(value, axis, pairs)


def fourier_tables(length):
    counter = np.arange(length)
    angles = 2.0 * np.pi / length * (counter[:, None] * counter[None, :] % length)
    cosine, sine = np.cos(angles), np.sin(angles)
    left_table = np.block([[cosine, sine], [-sine, cosine]])
    right_table = np.block([[cosine, -sine], [sine, cosine]])
    return [t.astype(np.float32).astype(ml_dtypes.bfloat16) for t in (left_table, right_table)]


def transform(real_part, imag_part, left_table, right_table):
    length = real_part.shape[0]
    stacked = jnp.concatenate([real_part, imag_part], 0).astype(jnp.bfloat16)
    inner = jnp.dot(left_table, stacked, preferred_element_type=jnp.float32).astype(jnp.bfloat16)
    beside = jnp.concatenate([inner[:length], inner[length:]], 1)
    outer = jnp.dot(beside, right_table, preferred_element_type=jnp.float32)
    return outer[:, :length], outer[:, length:]


def gradient_kernel(
    corners, own, right, lower, corner, probe, measured, left_table, right_table,
    main_out, right_out, lower_out, corner_out, field, grad,
):
    count, length = measured.shape[0], measured.shape[1]
    tile_px = own.shape[1]
    across, beyond = tile_px // LANES, length // LANES
    for part in range(2):
        for block in range(across):
            cols = slice(block * LANES, (block + 1) * LANES)
            field[part, block, :tile_px, :] = own[part, :, cols]
            field[part, block, tile_px:, :] = lower[part, :, cols]
        for block in range(beyond):
            cols = slice(block * LANES, (block + 1) * LANES)
            field[part, across + block, :tile_px, :] = right[part, :, cols]
            field[part, across + block, tile_px:, :] = corner[part, :, cols]
    grad[...] = jnp.zeros_like(grad)
    lane = lax.broadcasted_iota(jnp.int32, (length, LANES), 1)
    floor = (AMPLITUDE_FLOOR * length) ** 2

    def add_patch(number, carry):
        row, col = corners[number, 0], corners[number, 1]
        block, shift = col // LANES, col % LANES
        rows = pl.ds(row, length)
        head = lane < LANES - shift
        piece = []
        for part in range(2):
            turned = [
                pltpu.roll(field[part, block + i, rows, :], (LANES - shift) % LANES, 1)
                for i in range(beyond + 1)
            ]
            piece.append(
                jnp.concatenate(
                    [jnp.where(head, turned[i], turned[i + 1]) for i in range(beyond)], 1
                )
            )
        probe_real, probe_imag = probe[0], probe[1]
        exit_real = probe_real * piece[0] - probe_imag * piece[1]
        exit_imag = probe_real * piece[1] + probe_imag * piece[0]
        far_real, far_imag = transform(exit_real, exit_imag, left_table[...], right_table[...])
        power = jnp.maximum(far_real * far_real + far_imag * far_imag, floor)
        factor = measured[number].astype(jnp.float32) * (length * lax.rsqrt(power)) - 1.0
        back_real, back_imag = transform(
            factor * far_real, factor * far_imag, right_table[...], left_table[...]
        )
        terms = (
            probe_real * back_real + probe_imag * back_imag,
            probe_real * back_imag - probe_imag * back_real,
        )
        tail = lane >= shift
        for part in range(2):
            turned = [
                pltpu.roll(terms[part][:, i * LANES : (i + 1) * LANES], shift, 1)
                for i in range(beyond)
            ]
            grad[part, block, rows, :] += jnp.where(tail, turned[0], 0.0)
            for i in range(1, beyond):
                grad[part, block + i, rows, :] += jnp.where(tail, turned[i], turned[i - 1])
            grad[part, block + beyond, rows, :] += jnp.where(tail, 0.0, turned[beyond - 1])
        return carry

    lax.fori_loop(0, count, add_patch, 0)
    peak = jnp.max(probe[0] * probe[0] + probe[1] * probe[1], keepdims=True)
    scale = 1.0 / (peak * float(length * length))
    for part in range(2):
        for block in range(across):
            cols = slice(block * LANES, (block + 1) * LANES)
            main_out[part, :, cols] = own[part, :, cols] + grad[part, block, :tile_px, :] * scale
            lower_out[part, :, cols] = grad[part, block, tile_px:, :] * scale
        for block in range(beyond):
            cols = slice(block * LANES, (block + 1) * LANES)
            right_out[part, :, cols] = grad[part, across + block, :tile_px, :] * scale
            corner_out[part, :, cols] = grad[part, across + block, tile_px:, :] * scale


def patch_gradients(corners, own, right, lower, corner, probe, measured):
    count, length = measured.shape[0], measured.shape[1]
    tile_px = own.shape[1]
    left_table, right_table = (jnp.asarray(t) for t in fourier_tables(length))
    extent = tile_px + length
    vmem = pl.BlockSpec(memory_space=pltpu.VMEM)
    plane = pltpu.VMEM((2, extent // LANES, extent, LANES), jnp.float32)
    f32 = functools.partial(jax.ShapeDtypeStruct, dtype=jnp.float32)
    return pl.pallas_call(
        gradient_kernel,
        out_shape=[
            f32((2, tile_px, tile_px)),
            f32((2, tile_px, length)),
            f32((2, length, tile_px)),
            f32((2, length, length)),
        ],
        in_specs=[pl.BlockSpec(memory_space=pltpu.SMEM)] + [vmem] * 8,
        out_specs=[vmem] * 4,
        scratch_shapes=[plane, plane],
        compiler_params=pltpu.CompilerParams(vmem_limit_bytes=VMEM_BYTES),
        cost_estimate=pl.CostEstimate(
            flops=count * 32 * length**3, bytes_accessed=2**23, transcendentals=0
        ),
        name="patch_gradients",
    )(corners, own, right, lower, corner, probe, measured, left_table, right_table)


def fit_kernel(spectra, step, rate, data, fitted):
    energies, _, rows, width = data.shape
    materials = step.shape[0]
    cols = 2 * LANES
    blocks = width // cols

    def fit_block(number, carry):
        row = pl.multiple_of(number // blocks * 8, 8)
        col = pl.multiple_of(number % blocks * cols, cols)
        here = (pl.ds(row, 8), pl.ds(col, cols))
        target = [None] * materials
        for part in range(2):
            for energy in range(energies):
                value = data[(energy, part) + here]
                for m in range(materials):
                    term = spectra[part, energy * materials + m] * value
                    target[m] = term if target[m] is None else target[m] + term
        target = [rate[0] * value for value in target]
        start = tuple(jnp.maximum(value, 0.0) for value in target)

        def descend(number, coefficients):
            moved = []
            for m in range(materials):
                total = target[m]
                for n in range(materials):
                    total = total + step[m, n] * coefficients[n]
                moved.append(jnp.maximum(total, 0.0))
            return tuple(moved)

        coefficients = lax.fori_loop(1, FIT_STEPS, descend, start)
        for part in range(2):
            for energy in range(energies):
                total = spectra[part, energy * materials] * coefficients[0]
                for m in range(1, materials):
                    total = total + spectra[part, energy * materials + m] * coefficients[m]
                fitted[(energy, part) + here] = total
        return carry

    lax.fori_loop(0, rows // 8 * blocks, fit_block, 0)


def fit_spectra(data, materials):
    gram = jnp.einsum("rem,ren->mn", materials, materials, precision=lax.Precision.HIGHEST)
    rate = 1.0 / jnp.trace(gram)
    step = jnp.eye(gram.shape[0], dtype=jnp.float32) - rate * gram
    smem = pl.BlockSpec(memory_space=pltpu.SMEM)
    vmem = pl.BlockSpec(memory_space=pltpu.VMEM)
    return pl.pallas_call(
        fit_kernel,
        out_shape=jax.ShapeDtypeStruct(data.shape, jnp.float32),
        in_specs=[smem, smem, smem, vmem],
        out_specs=vmem,
        compiler_params=pltpu.CompilerParams(vmem_limit_bytes=VMEM_BYTES),
        name="fit_spectra",
    )(materials.reshape(2, -1), step, rate.reshape(1), data)


def body(object_tiles, probe_wave, measured, positions, materials):
    own = object_tiles[0, :, 0]
    tile_px = own.shape[-1]
    length = probe_wave.shape[-1]
    row_step = TILE_COLS % lax.axis_size("tile")
    right = shifted(own[:, :, :length], "tile", -1)
    lower = shifted(own[:, :length, :], "tile", -row_step)
    corner = shifted(lower[:, :, :length], "tile", -1)
    main, to_right, to_lower, to_corner = patch_gradients(
        positions[0], own, right, lower, corner, probe_wave[0], measured[0, 0]
    )
    from_left = shifted(to_right, "tile", 1)
    beside = shifted(to_corner, "tile", 1)
    lowered = jnp.concatenate([to_lower[:, :, :length] + beside, to_lower[:, :, length:]], 2)
    from_above = shifted(lowered, "tile", row_step)
    updated = (
        main
        + jnp.pad(from_left, ((0, 0), (0, 0), (0, tile_px - length)))
        + jnp.pad(from_above, ((0, 0), (0, tile_px - length), (0, 0)))
    )
    groups = lax.axis_size("energy")
    outgoing = updated.reshape(2, groups, tile_px // groups, tile_px).transpose(1, 0, 2, 3)
    arrived = lax.all_to_all(outgoing, "energy", split_axis=0, concat_axis=0, tiled=True)
    spectra = fit_spectra(arrived, materials)
    returned = lax.all_to_all(spectra, "energy", split_axis=0, concat_axis=0, tiled=True)
    return returned.transpose(1, 0, 2, 3).reshape(1, 2, 1, tile_px, tile_px)


def solution(mesh):
    in_specs = (
        P("energy", None, "tile", None, None),
        P("energy", None, None, None),
        P("energy", "tile", None, None, None),
        P("tile", None, None),
        P(),
    )
    out_specs = P("energy", None, "tile", None, None)
    return jax.shard_map(body, mesh=mesh, in_specs=in_specs, out_specs=out_specs, check_vma=False)
```

time: 681 us -> 319 us (0.47); the launches traced: 671 us -> 319 us
  local copies, waits for them, and re-layouts: 177 us -> 6.71 us
  matrix products: 101 us -> 0.76 us
  other arithmetic: 63.7 us -> 0.67 us
  loops' own time: 63 us -> 0 us
  starting transfers between devices: 29 us -> 91.1 us
  Pallas kernels: 0 us -> 40.6 us
  waiting for transfers between devices: 186 us -> 148 us
  blocking collectives: 52 us -> 30.6 us
    dynamic_update_slice x16 -> x0, local copies, waits for them, and re-layouts: 105 us -> none  [accumulate(): lax.dynamic_update_slice(gradient, current + jnp.stack([term_real, term_i...]
    dot_general x77 -> x1, matrix products: 101 us -> 0.76 us  [fit_spectra(): jnp.einsum('rem,ren->mn', materials, materials, precision=lax.Precision.H...]
    another operation x2 -> x0, loops' own time: 63 us -> none  [the longest x1 62.6 us: body(): gradient = lax.fori_loop(0, count, accumulate, jnp.zeros_like(extended))]
    ppermute x4 -> x6, starting transfers between devices: 24.5 us -> 84.3 us  [shifted(): return lax.ppermute(value, axis, pairs)]
    slice x50 -> x3, local copies, waits for them, and re-layouts: 46.5 us -> 3.42 us  [the longest x1 1.44 us: body(): lower = shifted(own[:, :length, :], 'tile', -row_step)]
    pallas_call x0 -> x2, Pallas kernels: none -> 40.6 us  [the longest x1 33.4 us: patch_gradients(): pl.pallas_call(gradient_kernel, out_shape=[f32((2, tile_px, tile_px)), f3...]
    ppermute x4 -> x6, waiting for transfers between devices: 137 us -> 101 us  [shifted(): return lax.ppermute(value, axis, pairs)]
    add x19 -> x2, other arithmetic: 27.8 us -> 0.53 us  [the longest x1 0.43 us: body(): main + jnp.pad(from_left, ((0, 0), (0, 0), (0, tile_px - length)))]
  transfers between devices with their start and end apart: 5 -> 7, of which waited for: 5 -> 5; matrix products, arithmetic and copies ran while one was open for 1% -> 1% of each run, Pallas kernels for 0% -> 0%
where the time goes in v1:
time: 319 us
  waiting for transfers between devices  148 us (46%)
  starting transfers between devices  91.1 us (29%)
  Pallas kernels  40.6 us (13%)
  blocking collectives  30.6 us (10%)
  local copies, waits for them, and re-layouts  6.71 us (2%)
    ppermute x6, waiting for transfers between devices, shifted(): return lax.ppermute(value, axis, pairs)  101 us
    ppermute x6, starting transfers between devices, shifted(): return lax.ppermute(value, axis, pairs)  84.3 us
    all_to_all x1, waiting for transfers between devices, body(): lax.all_to_all(outgoing, 'energy', split_axis=0, concat_axis=0, tiled=True)  47.1 us
    pallas_call x1, Pallas kernels, patch_gradients(): pl.pallas_call(gradient_kernel, out_shape=[f32((2, tile_px, tile_px)), f3...  33.4 us
    all_to_all x1, blocking collectives, body(): lax.all_to_all(spectra, 'energy', split_axis=0, concat_axis=0, tiled=True)  30.6 us
    pallas_call x1, Pallas kernels, fit_spectra(): pl.pallas_call(fit_kernel, out_shape=jax.ShapeDtypeStruct(data.shape, jnp...  7.2 us
    all_to_all x1, starting transfers between devices, body(): lax.all_to_all(outgoing, 'energy', split_axis=0, concat_axis=0, tiled=True)  6.79 us
  transfers between devices with their start and end apart: 7, of which 5 were waited for; matrix products, arithmetic and copies ran while one was open for 1% of the time, Pallas kernels for 0%

profile of v1, /device:TPU:9, one launch (start us, length us, event | category | flops | bytes accessed | tf_op | source)
XLA Modules:
  0.0 319.1 jit_solution(5050303722414565279)
XLA Ops:
  0.0 1.4 slice.21
  1.4 0.0 copy-start.7
  1.5 0.0 copy-start
  1.5 0.0 copy-start.1
  1.5 0.0 copy-start.2
  1.5 8.7 %collective-permute-start.1 = (f32[2,256,512]{2,1,0:T(8,128)S(1)}, f32[2,256,512]{2,1,0:T(8,128)S(1)}, u32[]{:S(2)}, u32[]{:S(2)}) collective-permute-start(f32[2,256,512]{2,1,0:T(8,128)S(1)} %slice.21), channel_id=1, source_target_pairs={{0,12},{1,13},{2,14},{3,15},{4,0},{5,1},{6,2},{7,3},{8,4},{9,5},{1... | collective-permute-start | bytes 3145736 | tf_op jit(solution)/shard_map/ppermute | solution.py:22
  10.2 1.1 slice.20
  11.3 1.0 collective-permute-start
  12.2 42.2 %collective-permute-done.1.lower = f32[2,256,512]{2,1,0:T(8,128)S(1)} collective-permute-done((f32[2,256,512]{2,1,0:T(8,128)S(1)}, f32[2,256,512]{2,1,0:T(8,128)S(1)}, u32[]{:S(2)}, u32[]{:S(2)}) %collective-permute-start.1) | collective-permute-done | bytes 1048608 | tf_op jit(solution)/shard_map/ppermute | solution.py:22
  54.5 0.9 slice.22
  55.4 1.7 collective-permute-start.2
  57.0 0.1 copy.11.corners
  57.1 0.0 collective-permute-done.right
  57.1 7.0 %collective-permute-done.2.corner = f32[2,256,256]{2,1,0:T(8,128)S(1)} collective-permute-done((f32[2,256,256]{2,1,0:T(8,128)}, f32[2,256,256]{2,1,0:T(8,128)S(1)}, u32[]{:S(2)}, u32[]{:S(2)}) %collective-permute-start.2) | collective-permute-done | bytes 524320 | tf_op jit(solution)/shard_map/ppermute | solution.py:22
  64.2 33.4 %patch_gradients.1 = (f32[2,512,512]{2,1,0:T(8,128)}, f32[2,512,256]{2,1,0:T(8,128)S(1)}, f32[2,256,512]{2,1,0:T(8,128)S(1)}, f32[2,256,256]{2,1,0:T(8,128)S(1)}) custom-call(s32[16,2]{1,0:T(8,128)S(1)} %copy.11.corners, f32[2,512,512]{2,1,0:T(8,128)} %bitcast.22, f32[2,512,256]{2,1,0:T(8,128)S(1)} %collective-permute-done.right, f32[2,256,512]{2,1,0:T(8,128)} %copy-done.5, ...), custom_call_target="tpu_custom_call" | custom-call | flops 8589934592 | bytes 8388608 | tf_op jit(solution)/shard_map/patch_gradients/pallas_call | solution.py:126
  97.6 0.0 collective-permute-start.4
  97.6 6.1 %collective-permute-done.4 = f32[2,256,256]{2,1,0:T(8,128)S(1)} collective-permute-done((f32[2,256,256]{2,1,0:T(8,128)S(1)}, f32[2,256,256]{2,1,0:T(8,128)S(1)}, u32[]{:S(2)}, u32[]{:S(2)}) %collective-permute-start.4) | collective-permute-done | bytes 524320 | tf_op jit(solution)/shard_map/ppermute | solution.py:22
  103.7 0.1 slice_add_fusion
  103.8 0.1 pad_maximum_fusion
  104.0 72.9 %collective-permute-start.5 = (f32[2,256,512]{2,1,0:T(8,128)S(1)}, f32[2,256,512]{2,1,0:T(8,128)S(1)}, u32[]{:S(2)}, u32[]{:S(2)}) collective-permute-start(f32[2,256,512]{2,1,0:T(8,128)S(1)} %pad_maximum_fusion), channel_id=1, source_target_pairs={{0,4},{1,5},{2,6},{3,7},{4,8},{5,9},{6,10},{7,11},{8,12},{9,13},{1... | collective-permute-start | bytes 3145736 | tf_op jit(solution)/shard_map/ppermute | solution.py:22
  176.9 0.0 collective-permute-done.3
  176.9 45.4 %collective-permute-done.5 = f32[2,256,512]{2,1,0:T(8,128)S(1)} collective-permute-done((f32[2,256,512]{2,1,0:T(8,128)S(1)}, f32[2,256,512]{2,1,0:T(8,128)S(1)}, u32[]{:S(2)}, u32[]{:S(2)}) %collective-permute-start.5) | collective-permute-done | bytes 1048608 | tf_op jit(solution)/shard_map/ppermute | solution.py:22
  222.3 0.4 pad_add_fusion
  222.8 1.5 copy.16
  224.2 6.8 %all-to-all-start = ((f32[16,2,32,512]{3,2,1,0:T(8,128)}), f32[16,2,32,512]{3,2,1,0:T(8,128)S(1)}, u32[]{:S(2)}, u32[]{:S(2)}) async-start(f32[16,2,32,512]{3,2,1,0:T(8,128)} %bitcast.19), calls=%async_computation | async-start | bytes 4194304 | tf_op jit(solution)/shard_map/all_to_all | solution.py:224
  231.1 0.1 copy.10
  231.1 0.1 reshape.12.spectra
  231.2 0.8 select_reduce_fusion
  232.7 47.1 %all-to-all-done.data = f32[16,2,32,512]{3,2,1,0:T(8,128)S(1)} async-done(((f32[16,2,32,512]{3,2,1,0:T(8,128)}), f32[16,2,32,512]{3,2,1,0:T(8,128)S(1)}, u32[]{:S(2)}, u32[]{:S(2)}) %all-to-all-start) | async-done | bytes 2097184 | tf_op jit(solution)/shard_map/all_to_all | solution.py:224
  279.7 7.2 %fit_spectra.1 = f32[16,2,32,512]{3,2,1,0:T(8,128)S(1)} custom-call(f32[2,128]{1,0:T(2,128)S(1)} %reshape.12.spectra, f32[8,8]{1,0:T(8,128)S(1)} %multiply_subtract_fusion.step, f32[1]{0:T(128)} %bitcast.1.rate, f32[16,2,32,512]{3,2,1,0:T(8,128)S(1)} %all-to-all-done.data), custom_call_target="tpu_custom_call" | custom-call | tf_op jit(solution)/shard_map/fit_spectra/pallas_call | solution.py:192
  286.9 30.6 %all_to_all.10 = f32[16,2,32,512]{3,2,1,0:T(8,128)S(1)} all-to-all(f32[16,2,32,512]{3,2,1,0:T(8,128)S(1)} %fit_spectra.1), channel_id=1, replica_groups=mesh['energy'=16,'tile'=16] {'energy'}, dimensions={0} | all-to-all | bytes 4194304 | tf_op jit(solution)/shard_map/all_to_all | solution.py:226
  317.6 1.5 copy.13
  (14 shorter events, 0.0 us)
Async XLA Ops:
  0.0 10.2 %copy-start.4 = (f32[1,2,1,512,512]{4,3,2,1,0:T(8,128)S(1)}, f32[1,2,1,512,512]{4,3,2,1,0:T(8,128)}, u32[]{:S(2)}) copy-start(f32[1,2,1,512,512]{4,3,2,1,0:T(8,128)} %param.7) | copy-start | bytes 6291460
  1.4 55.6 %copy-start.7 = (s32[1,16,2]{1,2,0:T(2,128)S(1)}, s32[1,16,2]{1,2,0:T(2,128)}, u32[]{:S(2)}) copy-start(s32[1,16,2]{1,2,0:T(2,128)} %param.10) | copy-start | bytes 388
  1.5 62.7 %copy-start = (f32[1,2,256,256]{3,2,1,0:T(8,128)S(1)}, f32[1,2,256,256]{3,2,1,0:T(8,128)}, u32[]{:S(2)}) copy-start(f32[1,2,256,256]{3,2,1,0:T(8,128)} %param.8) | copy-start | bytes 1572868
  1.5 62.7 %copy-start.1 = (bf16[512,512]{1,0:T(8,128)(2,1)S(1)}, bf16[512,512]{1,0:T(8,128)(2,1)}, u32[]{:S(2)}) copy-start(bf16[512,512]{1,0:T(8,128)(2,1)} %constant.13.clone.left_table) | copy-start | bytes 1572868
  1.5 62.7 %copy-start.2 = (bf16[512,512]{1,0:T(8,128)(2,1)S(1)}, bf16[512,512]{1,0:T(8,128)(2,1)}, u32[]{:S(2)}) copy-start(bf16[512,512]{1,0:T(8,128)(2,1)} %constant.14.clone.right_table) | copy-start | bytes 1572868
  1.5 53.0 %collective-permute-start.1 = (f32[2,256,512]{2,1,0:T(8,128)S(1)}, f32[2,256,512]{2,1,0:T(8,128)S(1)}, u32[]{:S(2)}, u32[]{:S(2)}) collective-permute-start(f32[2,256,512]{2,1,0:T(8,128)S(1)} %slice.21), channel_id=1, source_target_pairs={{0,12},{1,13},{2,14},{3,15},{4,0},{5,1},{6,2},{7,3},{8,4},{9,5},{1... | collective-permute-start | bytes 3145736 | tf_op jit(solution)/shard_map/ppermute | solution.py:22
  11.3 45.8 %collective-permute-start = (f32[2,512,256]{2,1,0:T(8,128)}, f32[2,512,256]{2,1,0:T(8,128)S(1)}, u32[]{:S(2)}, u32[]{:S(2)}) collective-permute-start(f32[2,512,256]{2,1,0:T(8,128)} %slice.20), channel_id=1, source_target_pairs={{0,15},{1,0},{2,1},{3,2},{4,3},{5,4},{6,5},{7,6},{8,7},{9,8},{10,9... | collective-permute-start | bytes 3145736 | tf_op jit(solution)/shard_map/ppermute | solution.py:22
  54.5 2.6 copy-start.5
  55.4 8.8 %collective-permute-start.2 = (f32[2,256,256]{2,1,0:T(8,128)}, f32[2,256,256]{2,1,0:T(8,128)S(1)}, u32[]{:S(2)}, u32[]{:S(2)}) collective-permute-start(f32[2,256,256]{2,1,0:T(8,128)} %slice.22), channel_id=1, source_target_pairs={{0,15},{1,0},{2,1},{3,2},{4,3},{5,4},{6,5},{7,6},{8,7},{9,8},{10,9... | collective-permute-start | bytes 1572872 | tf_op jit(solution)/shard_map/ppermute | solution.py:22
  97.6 6.1 %collective-permute-start.4 = (f32[2,256,256]{2,1,0:T(8,128)S(1)}, f32[2,256,256]{2,1,0:T(8,128)S(1)}, u32[]{:S(2)}, u32[]{:S(2)}) collective-permute-start(f32[2,256,256]{2,1,0:T(8,128)S(1)} %get-tuple-element.12), channel_id=1, source_target_pairs={{0,1},{1,2},{2,3},{3,4},{4,5},{5,6},{6,7},{7,8},{8,9},{9,10},{10,1... | collective-permute-start | bytes 1572872 | tf_op jit(solution)/shard_map/ppermute | solution.py:22
  97.6 79.3 %collective-permute-start.3 = (f32[2,512,256]{2,1,0:T(8,128)S(1)}, f32[2,512,256]{2,1,0:T(8,128)S(1)}, u32[]{:S(2)}, u32[]{:S(2)}) collective-permute-start(f32[2,512,256]{2,1,0:T(8,128)S(1)} %get-tuple-element.10), channel_id=1, source_target_pairs={{0,1},{1,2},{2,3},{3,4},{4,5},{5,6},{6,7},{7,8},{8,9},{9,10},{10,1... | collective-permute-start | bytes 3145736 | tf_op jit(solution)/shard_map/ppermute | solution.py:22
  103.7 118.6 %copy-start.3 = (f32[2,512,512]{2,1,0:T(8,128)S(1)}, f32[2,512,512]{2,1,0:T(8,128)}, u32[]{:S(2)}) copy-start(f32[2,512,512]{2,1,0:T(8,128)} %get-tuple-element.9) | copy-start | bytes 6291460
  104.0 118.3 %collective-permute-start.5 = (f32[2,256,512]{2,1,0:T(8,128)S(1)}, f32[2,256,512]{2,1,0:T(8,128)S(1)}, u32[]{:S(2)}, u32[]{:S(2)}) collective-permute-start(f32[2,256,512]{2,1,0:T(8,128)S(1)} %pad_maximum_fusion), channel_id=1, source_target_pairs={{0,4},{1,5},{2,6},{3,7},{4,8},{5,9},{6,10},{7,11},{8,12},{9,13},{1... | collective-permute-start | bytes 3145736 | tf_op jit(solution)/shard_map/ppermute | solution.py:22
  224.2 6.8 %copy-start.6 = (f32[2,16,8]{1,2,0:T(8,128)S(1)}, f32[2,16,8]{1,2,0:T(8,128)}, u32[]{:S(2)}) copy-start(f32[2,16,8]{1,2,0:T(8,128)} %param.11) | copy-start | bytes 3076
  224.2 55.5 %all-to-all-start = ((f32[16,2,32,512]{3,2,1,0:T(8,128)}), f32[16,2,32,512]{3,2,1,0:T(8,128)S(1)}, u32[]{:S(2)}, u32[]{:S(2)}) async-start(f32[16,2,32,512]{3,2,1,0:T(8,128)} %bitcast.19), calls=%async_computation | async-start | bytes 4194304 | tf_op jit(solution)/shard_map/all_to_all | solution.py:224

commit v2 on v1

--- a/solution.py
+++ b/solution.py
@@ -1,4 +1,5 @@
 import functools
+import math
 
 import jax
 import jax.numpy as jnp
@@ -13,13 +14,8 @@
 FIT_STEPS = 10
 AMPLITUDE_FLOOR = 0.5
 LANES = 128
+GROUP = 4
 VMEM_BYTES = 48 * 2**20
-
-
-def shifted(value, axis, steps):
-    count = lax.axis_size(axis)
-    pairs = [(source, (source + steps) % count) for source in range(count)]
-    return lax.ppermute(value, axis, pairs)
 
 
 def fourier_tables(length):
@@ -31,18 +27,25 @@
     return [t.astype(np.float32).astype(ml_dtypes.bfloat16) for t in (left_table, right_table)]
 
 
-def transform(real_part, imag_part, left_table, right_table):
-    length = real_part.shape[0]
-    stacked = jnp.concatenate([real_part, imag_part], 0).astype(jnp.bfloat16)
-    inner = jnp.dot(left_table, stacked, preferred_element_type=jnp.float32).astype(jnp.bfloat16)
-    beside = jnp.concatenate([inner[:length], inner[length:]], 1)
-    outer = jnp.dot(beside, right_table, preferred_element_type=jnp.float32)
-    return outer[:, :length], outer[:, length:]
+def times(left, right):
+    return jnp.dot(left, right, preferred_element_type=jnp.float32)
+
+
+def transforms(stacked, left_table, right_table):
+    length = stacked[0].shape[1]
+    inner = [times(left_table, value).astype(jnp.bfloat16) for value in stacked]
+    beside = [jnp.concatenate([value[:length], value[length:]], 1) for value in inner]
+    return [times(value, right_table) for value in beside]
+
+
+def stack(real_part, imag_part):
+    return jnp.concatenate([real_part.astype(jnp.bfloat16), imag_part.astype(jnp.bfloat16)], 0)
 
 
 def gradient_kernel(
-    corners, own, right, lower, corner, probe, measured, left_table, right_table,
-    main_out, right_out, lower_out, corner_out, field, grad,
+    corners, own, right, right_far, lower_left, lower_right, corner, corner_far, probe, measured,
+    left_table, right_table, main_out, right_out, lower_left_out, lower_right_out, corner_out,
+    field, grad,
 ):
     count, length = measured.shape[0], measured.shape[1]
     tile_px = own.shape[1]
@@ -51,19 +54,24 @@
         for block in range(across):
             cols = slice(block * LANES, (block + 1) * LANES)
             field[part, block, :tile_px, :] = own[part, :, cols]
-            field[part, block, tile_px:, :] = lower[part, :, cols]
         for block in range(beyond):
             cols = slice(block * LANES, (block + 1) * LANES)
-            field[part, across + block, :tile_px, :] = right[part, :, cols]
-            field[part, across + block, tile_px:, :] = corner[part, :, cols]
+            field[part, block, tile_px:, :] = lower_left[part, :, cols]
+            field[part, beyond + block, tile_px:, :] = lower_right[part, :, cols]
+            field[part, across + block, :tile_px, :] = right[part, :, cols] + right_far[part, :, cols]
+            field[part, across + block, tile_px:, :] = (
+                corner[part, :, cols] + corner_far[part, :, cols]
+            )
     grad[...] = jnp.zeros_like(grad)
     lane = lax.broadcasted_iota(jnp.int32, (length, LANES), 1)
     floor = (AMPLITUDE_FLOOR * length) ** 2
 
-    def add_patch(number, carry):
+    def place(number):
         row, col = corners[number, 0], corners[number, 1]
-        block, shift = col // LANES, col % LANES
-        rows = pl.ds(row, length)
+        return pl.ds(row, length), col // LANES, col % LANES
+
+    def exit_wave(number):
+        rows, block, shift = place(number)
         head = lane < LANES - shift
         piece = []
         for part in range(2):
@@ -77,14 +85,21 @@
                 )
             )
         probe_real, probe_imag = probe[0], probe[1]
-        exit_real = probe_real * piece[0] - probe_imag * piece[1]
-        exit_imag = probe_real * piece[1] + probe_imag * piece[0]
-        far_real, far_imag = transform(exit_real, exit_imag, left_table[...], right_table[...])
+        return stack(
+            probe_real * piece[0] - probe_imag * piece[1],
+            probe_real * piece[1] + probe_imag * piece[0],
+        )
+
+    def change(number, far):
+        far_real, far_imag = far[:, :length], far[:, length:]
         power = jnp.maximum(far_real * far_real + far_imag * far_imag, floor)
         factor = measured[number].astype(jnp.float32) * (length * lax.rsqrt(power)) - 1.0
-        back_real, back_imag = transform(
-            factor * far_real, factor * far_imag, right_table[...], left_table[...]
-        )
+        return stack(factor * far_real, factor * far_imag)
+
+    def add_terms(number, back):
+        rows, block, shift = place(number)
+        probe_real, probe_imag = probe[0], probe[1]
+        back_real, back_imag = back[:, :length], back[:, length:]
         terms = (
             probe_real * back_real + probe_imag * back_imag,
             probe_real * back_imag - probe_imag * back_real,
@@ -99,23 +114,35 @@
             for i in range(1, beyond):
                 grad[part, block + i, rows, :] += jnp.where(tail, turned[i], turned[i - 1])
             grad[part, block + beyond, rows, :] += jnp.where(tail, 0.0, turned[beyond - 1])
+
+    group = math.gcd(GROUP, count)
+
+    def add_group(first, carry):
+        numbers = [first * group + i for i in range(group)]
+        waves = [exit_wave(number) for number in numbers]
+        far = transforms(waves, left_table[...], right_table[...])
+        changes = [change(number, value) for number, value in zip(numbers, far)]
+        back = transforms(changes, right_table[...], left_table[...])
+        for number, value in zip(numbers, back):
+            add_terms(number, value)
         return carry
 
-    lax.fori_loop(0, count, add_patch, 0)
+    lax.fori_loop(0, count // group, add_group, 0)
     peak = jnp.max(probe[0] * probe[0] + probe[1] * probe[1], keepdims=True)
     scale = 1.0 / (peak * float(length * length))
     for part in range(2):
         for block in range(across):
             cols = slice(block * LANES, (block + 1) * LANES)
             main_out[part, :, cols] = own[part, :, cols] + grad[part, block, :tile_px, :] * scale
-            lower_out[part, :, cols] = grad[part, block, tile_px:, :] * scale
         for block in range(beyond):
             cols = slice(block * LANES, (block + 1) * LANES)
+            lower_left_out[part, :, cols] = grad[part, block, tile_px:, :] * scale
+            lower_right_out[part, :, cols] = grad[part, beyond + block, tile_px:, :] * scale
             right_out[part, :, cols] = grad[part, across + block, :tile_px, :] * scale
             corner_out[part, :, cols] = grad[part, across + block, tile_px:, :] * scale
 
 
-def patch_gradients(corners, own, right, lower, corner, probe, measured):
+def patch_gradients(corners, own, halos, probe, measured):
     count, length = measured.shape[0], measured.shape[1]
     tile_px = own.shape[1]
     left_table, right_table = (jnp.asarray(t) for t in fourier_tables(length))
@@ -123,23 +150,21 @@
     vmem = pl.BlockSpec(memory_space=pltpu.VMEM)
     plane = pltpu.VMEM((2, extent // LANES, extent, LANES), jnp.float32)
     f32 = functools.partial(jax.ShapeDtypeStruct, dtype=jnp.float32)
+    square = f32((2, length, length))
     return pl.pallas_call(
         gradient_kernel,
         out_shape=[
-            f32((2, tile_px, tile_px)),
-            f32((2, tile_px, length)),
-            f32((2, length, tile_px)),
-            f32((2, length, length)),
+            f32((2, tile_px, tile_px)), f32((2, tile_px, length)), square, square, square,
         ],
-        in_specs=[pl.BlockSpec(memory_space=pltpu.SMEM)] + [vmem] * 8,
-        out_specs=[vmem] * 4,
+        in_specs=[pl.BlockSpec(memory_space=pltpu.SMEM)] + [vmem] * 11,
+        out_specs=[vmem] * 5,
         scratch_shapes=[plane, plane],
         compiler_params=pltpu.CompilerParams(vmem_limit_bytes=VMEM_BYTES),
         cost_estimate=pl.CostEstimate(
             flops=count * 32 * length**3, bytes_accessed=2**23, transcendentals=0
         ),
         name="patch_gradients",
-    )(corners, own, right, lower, corner, probe, measured, left_table, right_table)
+    )(corners, own, *halos, probe, measured, left_table, right_table)
 
 
 def fit_kernel(spectra, step, rate, data, fitted):
@@ -203,21 +228,39 @@
     own = object_tiles[0, :, 0]
     tile_px = own.shape[-1]
     length = probe_wave.shape[-1]
-    row_step = TILE_COLS % lax.axis_size("tile")
-    right = shifted(own[:, :, :length], "tile", -1)
-    lower = shifted(own[:, :length, :], "tile", -row_step)
-    corner = shifted(lower[:, :, :length], "tile", -1)
-    main, to_right, to_lower, to_corner = patch_gradients(
-        positions[0], own, right, lower, corner, probe_wave[0], measured[0, 0]
-    )
-    from_left = shifted(to_right, "tile", 1)
-    beside = shifted(to_corner, "tile", 1)
-    lowered = jnp.concatenate([to_lower[:, :, :length] + beside, to_lower[:, :, length:]], 2)
-    from_above = shifted(lowered, "tile", row_step)
+    tiles = lax.axis_size("tile")
+    half = tiles // 2
+    last = half - 1
+
+    def move(value, pairs):
+        return lax.ppermute(value, "tile", [(s % tiles, d % tiles) for s, d in pairs])
+
+    lower_left = move(own[:, :length, :length], [(t, t - TILE_COLS) for t in range(tiles)])
+    right_step = move(own[:, :, :length], [(0, last), (half, half + last)])
+    corner_step = move(
+        own[:, :length, :length], [(TILE_COLS, half + TILE_COLS), (half + TILE_COLS, TILE_COLS)]
+    )
+    right = move(own[:, :, :length], [(t, t - 1) for t in range(tiles) if t % half])
+    lower_right = move(own[:, :length, length:], [(t, t - TILE_COLS) for t in range(tiles)])
+    right_far = move(right_step, [(last, half + last), (half + last, last)])
+    corner_far = move(corner_step, [(TILE_COLS, last), (half + TILE_COLS, half + last)])
+    corner = move(lower_left, [(t, t - 1) for t in range(tiles) if t % half])
+
+    halos = (right, right_far, lower_left, lower_right, corner, corner_far)
+    main, to_right, to_lower_left, to_lower_right, to_corner = patch_gradients(
+        positions[0], own, halos, probe_wave[0], measured[0, 0]
+    )
+    beside = move(to_corner, [(t, t + 1) for t in range(tiles)])
+    above_right = move(to_lower_right, [(t, t + TILE_COLS) for t in range(tiles)])
+    left_step = move(to_right, [(last, 0), (half + last, half)])
+    left = move(to_right, [(t, t + 1) for t in range(tiles) if t % half != last])
+    left_far = move(left_step, [(0, half), (half, 0)])
+    above_left = move(to_lower_left + beside, [(t, t + TILE_COLS) for t in range(tiles)])
+    above = jnp.concatenate([above_left, above_right], 2)
     updated = (
         main
-        + jnp.pad(from_left, ((0, 0), (0, 0), (0, tile_px - length)))
-        + jnp.pad(from_above, ((0, 0), (0, tile_px - length), (0, 0)))
+        + jnp.pad(left + left_far, ((0, 0), (0, 0), (0, tile_px - length)))
+        + jnp.pad(above, ((0, 0), (0, tile_px - length), (0, 0)))
     )
     groups = lax.axis_size("energy")
     outgoing = updated.reshape(2, groups, tile_px // groups, tile_px).transpose(1, 0, 2, 3)

time: 319 us -> 266 us (0.83)
  waiting for transfers between devices: 148 us -> 93.9 us
  blocking collectives: 30.6 us -> 52.5 us
  Pallas kernels: 40.6 us -> 26.7 us
  starting transfers between devices: 91.1 us -> 80.9 us
    ppermute x6 -> x14, waiting for transfers between devices: 101 us -> 49 us  [move(): lax.ppermute(value, 'tile', [(s % tiles, d % tiles) for s, d in pairs])]
    all_to_all x1, blocking collectives: 30.6 us -> 52.5 us  [body(): lax.all_to_all(spectra, 'energy', split_axis=0, concat_axis=0, tiled=True)]
    pallas_call x1, Pallas kernels: 33.4 us -> 19.5 us  [patch_gradients(): pl.pallas_call(gradient_kernel, out_shape=[f32((2, tile_px, tile_px)), f3...]
    ppermute x6 -> x14, starting transfers between devices: 84.3 us -> 76.7 us  [move(): lax.ppermute(value, 'tile', [(s % tiles, d % tiles) for s, d in pairs])]
  transfers between devices with their start and end apart: 7 -> 15, of which waited for: 5 -> 6; matrix products, arithmetic and copies ran while one was open for 1% -> 1% of each run, Pallas kernels for 0% -> 0%
where the time goes in v2:
time: 266 us; the launch traced here: 264 us
  waiting for transfers between devices  93.9 us (35%)
  starting transfers between devices  80.9 us (30%)
  blocking collectives  52.5 us (20%)
  Pallas kernels  26.7 us (10%)
  local copies, waits for them, and re-layouts  7.62 us (3%)
    ppermute x14, starting transfers between devices, move(): lax.ppermute(value, 'tile', [(s % tiles, d % tiles) for s, d in pairs])  76.7 us
    all_to_all x1, blocking collectives, body(): lax.all_to_all(spectra, 'energy', split_axis=0, concat_axis=0, tiled=True)  52.5 us
    ppermute x14, waiting for transfers between devices, move(): lax.ppermute(value, 'tile', [(s % tiles, d % tiles) for s, d in pairs])  49 us
    all_to_all x1, waiting for transfers between devices, body(): lax.all_to_all(outgoing, 'energy', split_axis=0, concat_axis=0, tiled=True)  44.9 us
    pallas_call x1, Pallas kernels, patch_gradients(): pl.pallas_call(gradient_kernel, out_shape=[f32((2, tile_px, tile_px)), f3...  19.5 us
    pallas_call x1, Pallas kernels, fit_spectra(): pl.pallas_call(fit_kernel, out_shape=jax.ShapeDtypeStruct(data.shape, jnp...  7.2 us
  transfers between devices with their start and end apart: 15, of which 6 were waited for; matrix products, arithmetic and copies ran while one was open for 1% of the time, Pallas kernels for 0%

profile of v2, /device:TPU:9, one launch (start us, length us, event | category | flops | bytes accessed | tf_op | source)
XLA Modules:
  0.0 263.9 jit_solution(16067590298506052490)
XLA Ops:
  0.0 2.4 slice.14
  2.4 1.7 collective-permute-start.1
  4.1 0.9 fusion.1
  5.0 8.3 %collective-permute-start.3 = (f32[2,256,256]{2,1,0:T(8,128)S(1)}, f32[2,256,256]{2,1,0:T(8,128)S(1)}, u32[]{:S(2)}, u32[]{:S(2)}) collective-permute-start(f32[2,256,256]{2,1,0:T(8,128)S(1)} %get-tuple-element.16), channel_id=1, source_target_pairs={{0,12},{1,13},{2,14},{3,15},{4,0},{5,1},{6,2},{7,3},{8,4},{9,5},{1... | collective-permute-start | bytes 1572872 | tf_op jit(solution)/shard_map/ppermute | solution.py:236
  13.3 1.4 collective-permute-start.6
  14.7 3.2 %collective-permute-start = (f32[2,512,256]{2,1,0:T(8,128)}, f32[2,512,256]{2,1,0:T(8,128)}, u32[]{:S(2)}, u32[]{:S(2)}) collective-permute-start(f32[2,512,256]{2,1,0:T(8,128)} %slice.14), channel_id=1, source_target_pairs={{1,0},{2,1},{3,2},{4,3},{5,4},{6,5},{7,6},{9,8},{10,9},{11,10},{12... | collective-permute-start | bytes 3145736 | tf_op jit(solution)/shard_map/ppermute | solution.py:236
  17.9 1.6 collective-permute-start.2
  19.6 26.6 %collective-permute-start.4 = (f32[2,256,256]{2,1,0:T(8,128)}, f32[2,256,256]{2,1,0:T(8,128)S(1)}, u32[]{:S(2)}, u32[]{:S(2)}) collective-permute-start(f32[2,256,256]{2,1,0:T(8,128)} %get-tuple-element.15), channel_id=1, source_target_pairs={{0,12},{1,13},{2,14},{3,15},{4,0},{5,1},{6,2},{7,3},{8,4},{9,5},{1... | collective-permute-start | bytes 1572872 | tf_op jit(solution)/shard_map/ppermute | solution.py:236
  46.2 1.9 collective-permute-start.5
  48.1 0.7 collective-permute-start.7
  48.9 9.9 %collective-permute-done.4.lower_right = f32[2,256,256]{2,1,0:T(8,128)S(1)} collective-permute-done((f32[2,256,256]{2,1,0:T(8,128)}, f32[2,256,256]{2,1,0:T(8,128)S(1)}, u32[]{:S(2)}, u32[]{:S(2)}) %collective-permute-start.4) | collective-permute-done | bytes 524320 | tf_op jit(solution)/shard_map/ppermute | solution.py:236
  58.9 1.0 copy-done.2
  60.0 19.5 %patch_gradients.1 = (f32[2,512,512]{2,1,0:T(8,128)}, f32[2,512,256]{2,1,0:T(8,128)}, f32[2,256,256]{2,1,0:T(8,128)S(1)}, f32[2,256,256]{2,1,0:T(8,128)S(1)}, f32[2,256,256]{2,1,0:T(8,128)S(1)}) custom-call(s32[16,2]{1,0:T(8,128)S(1)} %copy.11.corners, f32[2,512,512]{2,1,0:T(8,128)} %bitcast.22, f32[2,512,256]{2,1,0:T(8,128)} %collective-permute-done.right, ...), custom_call_target="tpu_custom_call" | custom-call | flops 8589934592 | bytes 8388608 | tf_op jit(solution)/shard_map/patch_gradients/pallas_call | solution.py:154
  79.4 0.7 collective-permute-start.9
  80.1 6.9 %collective-permute-start.8 = (f32[2,512,256]{2,1,0:T(8,128)}, f32[2,512,256]{2,1,0:T(8,128)S(1)}, u32[]{:S(2)}, u32[]{:S(2)}) collective-permute-start(f32[2,512,256]{2,1,0:T(8,128)} %get-tuple-element.11), channel_id=1, source_target_pairs={{0,1},{1,2},{2,3},{3,4},{4,5},{5,6},{6,7},{8,9},{9,10},{10,11},{11... | collective-permute-start | bytes 3145736 | tf_op jit(solution)/shard_map/ppermute | solution.py:236
  87.1 0.1 collective-permute-start.11
  87.2 0.7 collective-permute-start.10
  87.9 22.7 %collective-permute-start.13 = (f32[2,256,256]{2,1,0:T(8,128)S(1)}, f32[2,256,256]{2,1,0:T(8,128)S(1)}, u32[]{:S(2)}, u32[]{:S(2)}) collective-permute-start(f32[2,256,256]{2,1,0:T(8,128)S(1)} %get-tuple-element.14), channel_id=1, source_target_pairs={{0,4},{1,5},{2,6},{3,7},{4,8},{5,9},{6,10},{7,11},{8,12},{9,13},{1... | collective-permute-start | bytes 1572872 | tf_op jit(solution)/shard_map/ppermute | solution.py:236
  110.6 5.3 %collective-permute-done.11 = f32[2,256,256]{2,1,0:T(8,128)S(1)} collective-permute-done((f32[2,256,256]{2,1,0:T(8,128)S(1)}, f32[2,256,256]{2,1,0:T(8,128)S(1)}, u32[]{:S(2)}, u32[]{:S(2)}) %collective-permute-start.11) | collective-permute-done | bytes 524320 | tf_op jit(solution)/shard_map/ppermute | solution.py:236
  115.9 0.1 collective-permute-start.12
  116.0 0.1 add.16
  116.2 28.3 %collective-permute-done.13 = f32[2,256,256]{2,1,0:T(8,128)S(1)} collective-permute-done((f32[2,256,256]{2,1,0:T(8,128)S(1)}, f32[2,256,256]{2,1,0:T(8,128)S(1)}, u32[]{:S(2)}, u32[]{:S(2)}) %collective-permute-start.13) | collective-permute-done | bytes 524320 | tf_op jit(solution)/shard_map/ppermute | solution.py:236
  144.5 5.4 %collective-permute-done.12 = f32[2,256,256]{2,1,0:T(8,128)S(1)} collective-permute-done((f32[2,256,256]{2,1,0:T(8,128)S(1)}, f32[2,256,256]{2,1,0:T(8,128)S(1)}, u32[]{:S(2)}, u32[]{:S(2)}) %collective-permute-start.12) | collective-permute-done | bytes 524320 | tf_op jit(solution)/shard_map/ppermute | solution.py:236
  150.0 0.4 fusion
  150.3 1.5 copy.16
  151.8 4.3 %all-to-all-start = ((f32[16,2,32,512]{3,2,1,0:T(8,128)}), f32[16,2,32,512]{3,2,1,0:T(8,128)S(1)}, u32[]{:S(2)}, u32[]{:S(2)}) async-start(f32[16,2,32,512]{3,2,1,0:T(8,128)} %bitcast.19), calls=%async_computation | async-start | bytes 4194304 | tf_op jit(solution)/shard_map/all_to_all | solution.py:267
  156.2 0.1 reshape.12.spectra
  156.3 0.8 select_reduce_fusion
  157.8 44.9 %all-to-all-done.data = f32[16,2,32,512]{3,2,1,0:T(8,128)S(1)} async-done(((f32[16,2,32,512]{3,2,1,0:T(8,128)}), f32[16,2,32,512]{3,2,1,0:T(8,128)S(1)}, u32[]{:S(2)}, u32[]{:S(2)}) %all-to-all-start) | async-done | bytes 2097184 | tf_op jit(solution)/shard_map/all_to_all | solution.py:267
  202.7 7.2 %fit_spectra.1 = f32[16,2,32,512]{3,2,1,0:T(8,128)S(1)} custom-call(f32[2,128]{1,0:T(2,128)S(1)} %reshape.12.spectra, f32[8,8]{1,0:T(8,128)S(1)} %multiply_subtract_fusion.step, f32[1]{0:T(128)} %bitcast.1.rate, f32[16,2,32,512]{3,2,1,0:T(8,128)S(1)} %all-to-all-done.data), custom_call_target="tpu_custom_call" | custom-call | tf_op jit(solution)/shard_map/fit_spectra/pallas_call | solution.py:217
  209.9 52.5 %all_to_all.10 = f32[16,2,32,512]{3,2,1,0:T(8,128)S(1)} all-to-all(f32[16,2,32,512]{3,2,1,0:T(8,128)S(1)} %fit_spectra.1), channel_id=1, replica_groups=mesh['energy'=16,'tile'=16] {'energy'}, dimensions={0} | all-to-all | bytes 4194304 | tf_op jit(solution)/shard_map/all_to_all | solution.py:269
  262.4 1.5 copy.13
  (27 shorter events, 0.3 us)
Async XLA Ops:
  0.0 4.1 %copy-start.4 = (f32[1,2,1,512,512]{4,3,2,1,0:T(8,128)S(1)}, f32[1,2,1,512,512]{4,3,2,1,0:T(8,128)}, u32[]{:S(2)}) copy-start(f32[1,2,1,512,512]{4,3,2,1,0:T(8,128)} %param.7) | copy-start | bytes 6291460
  0.0 48.8 %copy-start.6 = (s32[1,16,2]{1,2,0:T(2,128)S(1)}, s32[1,16,2]{1,2,0:T(2,128)}, u32[]{:S(2)}) copy-start(s32[1,16,2]{1,2,0:T(2,128)} %param.10) | copy-start | bytes 388
  0.0 58.9 %copy-start = (f32[1,2,256,256]{3,2,1,0:T(8,128)S(1)}, f32[1,2,256,256]{3,2,1,0:T(8,128)}, u32[]{:S(2)}) copy-start(f32[1,2,256,256]{3,2,1,0:T(8,128)} %param.8) | copy-start | bytes 1572868
  0.0 58.9 %copy-start.1 = (bf16[512,512]{1,0:T(8,128)(2,1)S(1)}, bf16[512,512]{1,0:T(8,128)(2,1)}, u32[]{:S(2)}) copy-start(bf16[512,512]{1,0:T(8,128)(2,1)} %constant.13.clone.left_table) | copy-start | bytes 1572868
  2.4 15.5 %collective-permute-start.1 = (f32[2,512,256]{2,1,0:T(8,128)}, f32[2,512,256]{2,1,0:T(8,128)}, u32[]{:S(2)}, u32[]{:S(2)}) collective-permute-start(f32[2,512,256]{2,1,0:T(8,128)} %slice.14), channel_id=1, source_target_pairs={{0,7},{8,15},{16,23},{24,31},{32,39},{40,47},{48,55},{56,63},{64,7... | collective-permute-start | bytes 3145736 | tf_op jit(solution)/shard_map/ppermute | solution.py:236
  5.0 41.2 %collective-permute-start.3 = (f32[2,256,256]{2,1,0:T(8,128)S(1)}, f32[2,256,256]{2,1,0:T(8,128)S(1)}, u32[]{:S(2)}, u32[]{:S(2)}) collective-permute-start(f32[2,256,256]{2,1,0:T(8,128)S(1)} %get-tuple-element.16), channel_id=1, source_target_pairs={{0,12},{1,13},{2,14},{3,15},{4,0},{5,1},{6,2},{7,3},{8,4},{9,5},{1... | collective-permute-start | bytes 1572872 | tf_op jit(solution)/shard_map/ppermute | solution.py:236
  13.3 34.9 %collective-permute-start.6 = (f32[2,256,256]{2,1,0:T(8,128)S(1)}, f32[2,256,256]{2,1,0:T(8,128)}, u32[]{:S(2)}, u32[]{:S(2)}) collective-permute-start(f32[2,256,256]{2,1,0:T(8,128)S(1)} %get-tuple-element.16), channel_id=1, source_target_pairs={{4,12},{12,4},{20,28},{28,20},{36,44},{44,36},{52,60},{60,52},{68,... | collective-permute-start | bytes 1572872 | tf_op jit(solution)/shard_map/ppermute | solution.py:236
  14.7 44.2 %collective-permute-start = (f32[2,512,256]{2,1,0:T(8,128)}, f32[2,512,256]{2,1,0:T(8,128)}, u32[]{:S(2)}, u32[]{:S(2)}) collective-permute-start(f32[2,512,256]{2,1,0:T(8,128)} %slice.14), channel_id=1, source_target_pairs={{1,0},{2,1},{3,2},{4,3},{5,4},{6,5},{7,6},{9,8},{10,9},{11,10},{12... | collective-permute-start | bytes 3145736 | tf_op jit(solution)/shard_map/ppermute | solution.py:236
  17.9 41.0 %collective-permute-start.2 = (f32[2,512,256]{2,1,0:T(8,128)}, f32[2,512,256]{2,1,0:T(8,128)}, u32[]{:S(2)}, u32[]{:S(2)}) collective-permute-start(f32[2,512,256]{2,1,0:T(8,128)} %collective-permute-done.1), channel_id=1, source_target_pairs={{7,15},{15,7},{23,31},{31,23},{39,47},{47,39},{55,63},{63,55},{71,... | collective-permute-start | bytes 3145736 | tf_op jit(solution)/shard_map/ppermute | solution.py:236
  19.6 39.2 %collective-permute-start.4 = (f32[2,256,256]{2,1,0:T(8,128)}, f32[2,256,256]{2,1,0:T(8,128)S(1)}, u32[]{:S(2)}, u32[]{:S(2)}) collective-permute-start(f32[2,256,256]{2,1,0:T(8,128)} %get-tuple-element.15), channel_id=1, source_target_pairs={{0,12},{1,13},{2,14},{3,15},{4,0},{5,1},{6,2},{7,3},{8,4},{9,5},{1... | collective-permute-start | bytes 1572872 | tf_op jit(solution)/shard_map/ppermute | solution.py:236
  46.2 12.7 %collective-permute-start.5 = (f32[2,256,256]{2,1,0:T(8,128)S(1)}, f32[2,256,256]{2,1,0:T(8,128)S(1)}, u32[]{:S(2)}, u32[]{:S(2)}) collective-permute-start(f32[2,256,256]{2,1,0:T(8,128)S(1)} %collective-permute-done.3.lower_left), channel_id=1, source_target_pairs={{1,0},{2,1},{3,2},{4,3},{5,4},{6,5},{7,6},{9,8},{10,9},{11,10},{12... | collective-permute-start | bytes 1572872 | tf_op jit(solution)/shard_map/ppermute | solution.py:236
  48.1 10.7 %collective-permute-start.7 = (f32[2,256,256]{2,1,0:T(8,128)}, f32[2,256,256]{2,1,0:T(8,128)S(1)}, u32[]{:S(2)}, u32[]{:S(2)}) collective-permute-start(f32[2,256,256]{2,1,0:T(8,128)} %collective-permute-done.6), channel_id=1, source_target_pairs={{4,7},{12,15},{20,23},{28,31},{36,39},{44,47},{52,55},{60,63},{68,... | collective-permute-start | bytes 1572872 | tf_op jit(solution)/shard_map/ppermute | solution.py:236
  58.9 1.0 copy-start.2
  79.4 7.7 %collective-permute-start.9 = (f32[2,512,256]{2,1,0:T(8,128)}, f32[2,512,256]{2,1,0:T(8,128)S(1)}, u32[]{:S(2)}, u32[]{:S(2)}) collective-permute-start(f32[2,512,256]{2,1,0:T(8,128)} %get-tuple-element.11), channel_id=1, source_target_pairs={{7,0},{15,8},{23,16},{31,24},{39,32},{47,40},{55,48},{63,56},{71,6... | collective-permute-start | bytes 3145736 | tf_op jit(solution)/shard_map/ppermute | solution.py:236
  80.1 35.9 %collective-permute-start.8 = (f32[2,512,256]{2,1,0:T(8,128)}, f32[2,512,256]{2,1,0:T(8,128)S(1)}, u32[]{:S(2)}, u32[]{:S(2)}) collective-permute-start(f32[2,512,256]{2,1,0:T(8,128)} %get-tuple-element.11), channel_id=1, source_target_pairs={{0,1},{1,2},{2,3},{3,4},{4,5},{5,6},{6,7},{8,9},{9,10},{10,11},{11... | collective-permute-start | bytes 3145736 | tf_op jit(solution)/shard_map/ppermute | solution.py:236
  87.1 28.8 %collective-permute-start.11 = (f32[2,256,256]{2,1,0:T(8,128)S(1)}, f32[2,256,256]{2,1,0:T(8,128)S(1)}, u32[]{:S(2)}, u32[]{:S(2)}) collective-permute-start(f32[2,256,256]{2,1,0:T(8,128)S(1)} %get-tuple-element.13), channel_id=1, source_target_pairs={{0,1},{1,2},{2,3},{3,4},{4,5},{5,6},{6,7},{7,8},{8,9},{9,10},{10,1... | collective-permute-start | bytes 1572872 | tf_op jit(solution)/shard_map/ppermute | solution.py:236
  87.2 28.9 %collective-permute-start.10 = (f32[2,512,256]{2,1,0:T(8,128)S(1)}, f32[2,512,256]{2,1,0:T(8,128)S(1)}, u32[]{:S(2)}, u32[]{:S(2)}) collective-permute-start(f32[2,512,256]{2,1,0:T(8,128)S(1)} %collective-permute-done.9), channel_id=1, source_target_pairs={{0,8},{8,0},{16,24},{24,16},{32,40},{40,32},{48,56},{56,48},{64,72... | collective-permute-start | bytes 3145736 | tf_op jit(solution)/shard_map/ppermute | solution.py:236
  87.9 56.6 %collective-permute-start.13 = (f32[2,256,256]{2,1,0:T(8,128)S(1)}, f32[2,256,256]{2,1,0:T(8,128)S(1)}, u32[]{:S(2)}, u32[]{:S(2)}) collective-permute-start(f32[2,256,256]{2,1,0:T(8,128)S(1)} %get-tuple-element.14), channel_id=1, source_target_pairs={{0,4},{1,5},{2,6},{3,7},{4,8},{5,9},{6,10},{7,11},{8,12},{9,13},{1... | collective-permute-start | bytes 1572872 | tf_op jit(solution)/shard_map/ppermute | solution.py:236
  115.8 34.1 %copy-start.3 = (f32[2,512,512]{2,1,0:T(8,128)S(1)}, f32[2,512,512]{2,1,0:T(8,128)}, u32[]{:S(2)}) copy-start(f32[2,512,512]{2,1,0:T(8,128)} %get-tuple-element.10) | copy-start | bytes 6291460
  115.9 34.0 %collective-permute-start.12 = (f32[2,256,256]{2,1,0:T(8,128)S(1)}, f32[2,256,256]{2,1,0:T(8,128)S(1)}, u32[]{:S(2)}, u32[]{:S(2)}) collective-permute-start(f32[2,256,256]{2,1,0:T(8,128)S(1)} %add.18), channel_id=1, source_target_pairs={{0,4},{1,5},{2,6},{3,7},{4,8},{5,9},{6,10},{7,11},{8,12},{9,13},{1... | collective-permute-start | bytes 1572872 | tf_op jit(solution)/shard_map/ppermute | solution.py:236
  151.8 4.3 %copy-start.5 = (f32[2,16,8]{1,2,0:T(8,128)S(1)}, f32[2,16,8]{1,2,0:T(8,128)}, u32[]{:S(2)}) copy-start(f32[2,16,8]{1,2,0:T(8,128)} %param.11) | copy-start | bytes 3076
  151.8 50.8 %all-to-all-start = ((f32[16,2,32,512]{3,2,1,0:T(8,128)}), f32[16,2,32,512]{3,2,1,0:T(8,128)S(1)}, u32[]{:S(2)}, u32[]{:S(2)}) async-start(f32[16,2,32,512]{3,2,1,0:T(8,128)} %bitcast.19), calls=%async_computation | async-start | bytes 4194304 | tf_op jit(solution)/shard_map/all_to_all | solution.py:267

commit v3 on v2

--- a/solution.py
+++ b/solution.py
@@ -14,8 +14,9 @@
 FIT_STEPS = 10
 AMPLITUDE_FLOOR = 0.5
 LANES = 128
-GROUP = 4
-VMEM_BYTES = 48 * 2**20
+GROUP = 8
+VMEM_BYTES = 36 * 2**20
+SMALL_VMEM_BYTES = 16 * 2**20
 
 
 def fourier_tables(length):
@@ -167,6 +168,34 @@
     )(corners, own, *halos, probe, measured, left_table, right_table)
 
 
+def combine_kernel(main, left, left_far, above_left, above_right, outgoing):
+    groups, _, rows, _ = outgoing.shape
+    length = left.shape[2]
+    for group in range(groups):
+        here = slice(group * rows, (group + 1) * rows)
+        for part in range(2):
+            near = main[part, here, :length] + (left[part, here, :] + left_far[part, here, :])
+            far = main[part, here, length:]
+            if group * rows < length:
+                near = near + above_left[part, here, :]
+                far = far + above_right[part, here, :]
+            outgoing[group, part, :, :length] = near
+            outgoing[group, part, :, length:] = far
+
+
+def combine(main, left, left_far, above_left, above_right, groups):
+    tile_px = main.shape[1]
+    vmem = pl.BlockSpec(memory_space=pltpu.VMEM)
+    return pl.pallas_call(
+        combine_kernel,
+        out_shape=jax.ShapeDtypeStruct((groups, 2, tile_px // groups, tile_px), jnp.float32),
+        in_specs=[vmem] * 5,
+        out_specs=vmem,
+        compiler_params=pltpu.CompilerParams(vmem_limit_bytes=SMALL_VMEM_BYTES),
+        name="combine",
+    )(main, left, left_far, above_left, above_right)
+
+
 def fit_kernel(spectra, step, rate, data, fitted):
     energies, _, rows, width = data.shape
     materials = step.shape[0]
@@ -219,7 +248,7 @@
         out_shape=jax.ShapeDtypeStruct(data.shape, jnp.float32),
         in_specs=[smem, smem, smem, vmem],
         out_specs=vmem,
-        compiler_params=pltpu.CompilerParams(vmem_limit_bytes=VMEM_BYTES),
+        compiler_params=pltpu.CompilerParams(vmem_limit_bytes=SMALL_VMEM_BYTES),
         name="fit_spectra",
     )(materials.reshape(2, -1), step, rate.reshape(1), data)
 
@@ -240,30 +269,26 @@
     corner_step = move(
         own[:, :length, :length], [(TILE_COLS, half + TILE_COLS), (half + TILE_COLS, TILE_COLS)]
     )
-    right = move(own[:, :, :length], [(t, t - 1) for t in range(tiles) if t % half])
     lower_right = move(own[:, :length, length:], [(t, t - TILE_COLS) for t in range(tiles)])
+    right_step, columns = lax.optimization_barrier((right_step, own[:, :, :length]))
+    right = move(columns, [(t, t - 1) for t in range(tiles) if t % half])
     right_far = move(right_step, [(last, half + last), (half + last, last)])
+    corner = move(lower_left, [(t, t - 1) for t in range(tiles) if t % half])
     corner_far = move(corner_step, [(TILE_COLS, last), (half + TILE_COLS, half + last)])
-    corner = move(lower_left, [(t, t - 1) for t in range(tiles) if t % half])
 
     halos = (right, right_far, lower_left, lower_right, corner, corner_far)
     main, to_right, to_lower_left, to_lower_right, to_corner = patch_gradients(
         positions[0], own, halos, probe_wave[0], measured[0, 0]
     )
     beside = move(to_corner, [(t, t + 1) for t in range(tiles)])
+    left_step = move(to_right, [(last, 0), (half + last, half)])
     above_right = move(to_lower_right, [(t, t + TILE_COLS) for t in range(tiles)])
-    left_step = move(to_right, [(last, 0), (half + last, half)])
+    beside, to_right = lax.optimization_barrier((beside, to_right))
     left = move(to_right, [(t, t + 1) for t in range(tiles) if t % half != last])
+    above_left = move(to_lower_left + beside, [(t, t + TILE_COLS) for t in range(tiles)])
     left_far = move(left_step, [(0, half), (half, 0)])
-    above_left = move(to_lower_left + beside, [(t, t + TILE_COLS) for t in range(tiles)])
-    above = jnp.concatenate([above_left, above_right], 2)
-    updated = (
-        main
-        + jnp.pad(left + left_far, ((0, 0), (0, 0), (0, tile_px - length)))
-        + jnp.pad(above, ((0, 0), (0, tile_px - length), (0, 0)))
-    )
     groups = lax.axis_size("energy")
-    outgoing = updated.reshape(2, groups, tile_px // groups, tile_px).transpose(1, 0, 2, 3)
+    outgoing = combine(main, left, left_far, above_left, above_right, groups)
     arrived = lax.all_to_all(outgoing, "energy", split_axis=0, concat_axis=0, tiled=True)
     spectra = fit_spectra(arrived, materials)
     returned = lax.all_to_all(spectra, "energy", split_axis=0, concat_axis=0, tiled=True)

time: 266 us -> 275 us (1.034)
  waiting for transfers between devices: 93.9 us -> 114 us
  starting transfers between devices: 80.9 us -> 70.3 us
    ppermute x14, starting transfers between devices: 76.7 us -> 63.6 us  [move(): lax.ppermute(value, 'tile', [(s % tiles, d % tiles) for s, d in pairs])]
    ppermute x14, waiting for transfers between devices: 49 us -> 61.2 us  [move(): lax.ppermute(value, 'tile', [(s % tiles, d % tiles) for s, d in pairs])]
    all_to_all x1, waiting for transfers between devices: 44.9 us -> 53 us  [body(): lax.all_to_all(outgoing, 'energy', split_axis=0, concat_axis=0, tiled=True)]
    unnamed x15, local copies, waits for them, and re-layouts: 1.14 us -> 4.79 us
    pallas_call x1, Pallas kernels: 19.5 us -> 16.2 us  [patch_gradients(): pl.pallas_call(gradient_kernel, out_shape=[f32((2, tile_px, tile_px)), f3...]
where the time goes in v3:
time: 275 us; the launch traced here: 273 us
  waiting for transfers between devices  114 us (41%)
  starting transfers between devices  70.3 us (26%)
  blocking collectives  52 us (19%)
  Pallas kernels  25.1 us (9%)
  local copies, waits for them, and re-layouts  9.8 us (4%)
    ppermute x14, starting transfers between devices, move(): lax.ppermute(value, 'tile', [(s % tiles, d % tiles) for s, d in pairs])  63.6 us
    ppermute x14, waiting for transfers between devices, move(): lax.ppermute(value, 'tile', [(s % tiles, d % tiles) for s, d in pairs])  61.2 us
    all_to_all x1, waiting for transfers between devices, body(): lax.all_to_all(outgoing, 'energy', split_axis=0, concat_axis=0, tiled=True)  53 us
    all_to_all x1, blocking collectives, body(): lax.all_to_all(spectra, 'energy', split_axis=0, concat_axis=0, tiled=True)  52 us
    pallas_call x1, Pallas kernels, patch_gradients(): pl.pallas_call(gradient_kernel, out_shape=[f32((2, tile_px, tile_px)), f3...  16.2 us
    pallas_call x1, Pallas kernels, fit_spectra(): pl.pallas_call(fit_kernel, out_shape=jax.ShapeDtypeStruct(data.shape, jnp...  7.2 us
    all_to_all x1, starting transfers between devices, body(): lax.all_to_all(outgoing, 'energy', split_axis=0, concat_axis=0, tiled=True)  6.65 us
  transfers between devices with their start and end apart: 15, of which 6 were waited for; matrix products, arithmetic and copies ran while one was open for 1% of the time, Pallas kernels for 0%

profile of v3, /device:TPU:9, one launch (start us, length us, event | category | flops | bytes accessed | tf_op | source)
XLA Modules:
  0.0 273.1 jit_solution(12061964663354808944)
XLA Ops:
  0.0 2.4 slice.14
  2.4 1.7 collective-permute-start
  4.1 0.9 fusion
  5.0 8.3 %collective-permute-start.3 = (f32[2,256,256]{2,1,0:T(8,128)S(1)}, f32[2,256,256]{2,1,0:T(8,128)}, u32[]{:S(2)}, u32[]{:S(2)}) collective-permute-start(f32[2,256,256]{2,1,0:T(8,128)S(1)} %get-tuple-element.24), channel_id=1, source_target_pairs={{0,12},{1,13},{2,14},{3,15},{4,0},{5,1},{6,2},{7,3},{8,4},{9,5},{1... | collective-permute-start | bytes 1572872 | tf_op jit(solution)/shard_map/ppermute | solution.py:265
  13.3 1.4 collective-permute-start.6
  14.7 3.2 %collective-permute-start.1 = (f32[2,512,256]{2,1,0:T(8,128)}, f32[2,512,256]{2,1,0:T(8,128)S(1)}, u32[]{:S(2)}, u32[]{:S(2)}) collective-permute-start(f32[2,512,256]{2,1,0:T(8,128)} %slice.14), channel_id=1, source_target_pairs={{1,0},{2,1},{3,2},{4,3},{5,4},{6,5},{7,6},{9,8},{10,9},{11,10},{12... | collective-permute-start | bytes 3145736 | tf_op jit(solution)/shard_map/ppermute | solution.py:265
  17.9 1.6 collective-permute-start.2
  19.6 28.1 %collective-permute-start.4 = (f32[2,256,256]{2,1,0:T(8,128)}, f32[2,256,256]{2,1,0:T(8,128)}, u32[]{:S(2)}, u32[]{:S(2)}) collective-permute-start(f32[2,256,256]{2,1,0:T(8,128)} %get-tuple-element.23), channel_id=1, source_target_pairs={{0,12},{1,13},{2,14},{3,15},{4,0},{5,1},{6,2},{7,3},{8,4},{9,5},{1... | collective-permute-start | bytes 1572872 | tf_op jit(solution)/shard_map/ppermute | solution.py:265
  47.7 1.9 collective-permute-start.5
  49.6 1.5 collective-permute-start.7
  51.1 7.7 %collective-permute-done.4.lower_right = f32[2,256,256]{2,1,0:T(8,128)} collective-permute-done((f32[2,256,256]{2,1,0:T(8,128)}, f32[2,256,256]{2,1,0:T(8,128)}, u32[]{:S(2)}, u32[]{:S(2)}) %collective-permute-start.4) | collective-permute-done | bytes 524320 | tf_op jit(solution)/shard_map/ppermute | solution.py:265
  58.8 3.5 %collective-permute-done.5.corner = f32[2,256,256]{2,1,0:T(8,128)} collective-permute-done((f32[2,256,256]{2,1,0:T(8,128)}, f32[2,256,256]{2,1,0:T(8,128)}, u32[]{:S(2)}, u32[]{:S(2)}) %collective-permute-start.5) | collective-permute-done | bytes 524320 | tf_op jit(solution)/shard_map/ppermute | solution.py:265
  62.3 1.6 copy-done.1
  63.9 1.0 copy-done.2
  64.9 1.0 copy-done.3
  66.0 1.0 copy-done.4
  67.0 16.2 %patch_gradients.1 = (f32[2,512,512]{2,1,0:T(8,128)S(1)}, f32[2,512,256]{2,1,0:T(8,128)S(1)}, f32[2,256,256]{2,1,0:T(8,128)S(1)}, f32[2,256,256]{2,1,0:T(8,128)S(1)}, f32[2,256,256]{2,1,0:T(8,128)S(1)}) custom-call(s32[16,2]{1,0:T(8,128)S(1)} %copy.11.corners, f32[2,512,512]{2,1,0:T(8,128)S(1)} %bitcast.15, f32[2,512,256]{2,1,0:T(8,128)S(1)} %collective-permute-done.1.right, ...), custom_call_target="tpu_custom_call" | custom-call | flops 8589934592 | bytes 8388608 | tf_op jit(solution)/shard_map/patch_gradients/pallas_call | solution.py:155
  83.3 0.7 collective-permute-start.10
  84.0 2.6 collective-permute-start.8
  86.6 6.1 %collective-permute-done.8 = f32[2,256,256]{2,1,0:T(8,128)S(1)} collective-permute-done((f32[2,256,256]{2,1,0:T(8,128)S(1)}, f32[2,256,256]{2,1,0:T(8,128)S(1)}, u32[]{:S(2)}, u32[]{:S(2)}) %collective-permute-start.8) | collective-permute-done | bytes 524320 | tf_op jit(solution)/shard_map/ppermute | solution.py:265
  92.7 4.4 %collective-permute-start.9 = (f32[2,512,256]{2,1,0:T(8,128)S(1)}, f32[2,512,256]{2,1,0:T(8,128)S(1)}, u32[]{:S(2)}, u32[]{:S(2)}) collective-permute-start(f32[2,512,256]{2,1,0:T(8,128)S(1)} %get-tuple-element.19), channel_id=1, source_target_pairs={{0,1},{1,2},{2,3},{3,4},{4,5},{5,6},{6,7},{8,9},{9,10},{10,11},{11... | collective-permute-start | bytes 3145736 | tf_op jit(solution)/shard_map/ppermute | solution.py:265
  97.1 0.7 collective-permute-start.11
  97.8 7.4 %collective-permute-start.13 = (f32[2,256,256]{2,1,0:T(8,128)S(1)}, f32[2,256,256]{2,1,0:T(8,128)S(1)}, u32[]{:S(2)}, u32[]{:S(2)}) collective-permute-start(f32[2,256,256]{2,1,0:T(8,128)S(1)} %get-tuple-element.22), channel_id=1, source_target_pairs={{0,4},{1,5},{2,6},{3,7},{4,8},{5,9},{6,10},{7,11},{8,12},{9,13},{1... | collective-permute-start | bytes 1572872 | tf_op jit(solution)/shard_map/ppermute | solution.py:265
  105.4 32.8 %collective-permute-done.13.above_right = f32[2,256,256]{2,1,0:T(8,128)S(1)} collective-permute-done((f32[2,256,256]{2,1,0:T(8,128)S(1)}, f32[2,256,256]{2,1,0:T(8,128)S(1)}, u32[]{:S(2)}, u32[]{:S(2)}) %collective-permute-start.13) | collective-permute-done | bytes 524320 | tf_op jit(solution)/shard_map/ppermute | solution.py:265
  138.3 11.0 %collective-permute-done.12.above_left = f32[2,256,256]{2,1,0:T(8,128)S(1)} collective-permute-done((f32[2,256,256]{2,1,0:T(8,128)S(1)}, f32[2,256,256]{2,1,0:T(8,128)S(1)}, u32[]{:S(2)}, u32[]{:S(2)}) %collective-permute-start.12) | collective-permute-done | bytes 524320 | tf_op jit(solution)/shard_map/ppermute | solution.py:265
  149.3 1.7 combine.1
  151.0 6.6 %all-to-all-start = ((f32[16,2,32,512]{3,2,1,0:T(8,128)}), f32[16,2,32,512]{3,2,1,0:T(8,128)S(1)}, u32[]{:S(2)}, u32[]{:S(2)}) async-start(f32[16,2,32,512]{3,2,1,0:T(8,128)} %combine.1), calls=%async_computation | async-start | bytes 4194304 | tf_op jit(solution)/shard_map/all_to_all | solution.py:292
  157.8 0.8 select_reduce_fusion
  159.3 53.0 %all-to-all-done.data = f32[16,2,32,512]{3,2,1,0:T(8,128)S(1)} async-done(((f32[16,2,32,512]{3,2,1,0:T(8,128)}), f32[16,2,32,512]{3,2,1,0:T(8,128)S(1)}, u32[]{:S(2)}, u32[]{:S(2)}) %all-to-all-start) | async-done | bytes 2097184 | tf_op jit(solution)/shard_map/all_to_all | solution.py:292
  212.3 7.2 %fit_spectra.1 = f32[16,2,32,512]{3,2,1,0:T(8,128)S(1)} custom-call(f32[2,128]{1,0:T(2,128)S(1)} %reshape.9.spectra, f32[8,8]{1,0:T(8,128)S(1)} %multiply_subtract_fusion.step, f32[1]{0:T(128)} %bitcast.1.rate, f32[16,2,32,512]{3,2,1,0:T(8,128)S(1)} %all-to-all-done.data), custom_call_target="tpu_custom_call" | custom-call | tf_op jit(solution)/shard_map/fit_spectra/pallas_call | solution.py:246
  219.5 52.0 %all_to_all.10 = f32[16,2,32,512]{3,2,1,0:T(8,128)S(1)} all-to-all(f32[16,2,32,512]{3,2,1,0:T(8,128)S(1)} %fit_spectra.1), channel_id=1, replica_groups=mesh['energy'=16,'tile'=16] {'energy'}, dimensions={0} | all-to-all | bytes 4194304 | tf_op jit(solution)/shard_map/all_to_all | solution.py:294
  271.6 1.5 copy.12
  (25 shorter events, 0.5 us)
Async XLA Ops:
  0.0 4.1 %copy-start = (f32[1,2,1,512,512]{4,3,2,1,0:T(8,128)S(1)}, f32[1,2,1,512,512]{4,3,2,1,0:T(8,128)}, u32[]{:S(2)}) copy-start(f32[1,2,1,512,512]{4,3,2,1,0:T(8,128)} %param.7) | copy-start | bytes 6291460
  0.0 51.1 %copy-start.6 = (s32[1,16,2]{1,2,0:T(2,128)S(1)}, s32[1,16,2]{1,2,0:T(2,128)}, u32[]{:S(2)}) copy-start(s32[1,16,2]{1,2,0:T(2,128)} %param.10) | copy-start | bytes 388
  2.4 12.3 %collective-permute-start = (f32[2,512,256]{2,1,0:T(8,128)}, f32[2,512,256]{2,1,0:T(8,128)}, u32[]{:S(2)}, u32[]{:S(2)}) collective-permute-start(f32[2,512,256]{2,1,0:T(8,128)} %slice.14), channel_id=1, source_target_pairs={{0,7},{8,15},{16,23},{24,31},{32,39},{40,47},{48,55},{56,63},{64,7... | collective-permute-start | bytes 3145736 | tf_op jit(solution)/shard_map/ppermute | solution.py:265
  5.0 42.7 %collective-permute-start.3 = (f32[2,256,256]{2,1,0:T(8,128)S(1)}, f32[2,256,256]{2,1,0:T(8,128)}, u32[]{:S(2)}, u32[]{:S(2)}) collective-permute-start(f32[2,256,256]{2,1,0:T(8,128)S(1)} %get-tuple-element.24), channel_id=1, source_target_pairs={{0,12},{1,13},{2,14},{3,15},{4,0},{5,1},{6,2},{7,3},{8,4},{9,5},{1... | collective-permute-start | bytes 1572872 | tf_op jit(solution)/shard_map/ppermute | solution.py:265
  13.3 36.3 %collective-permute-start.6 = (f32[2,256,256]{2,1,0:T(8,128)S(1)}, f32[2,256,256]{2,1,0:T(8,128)}, u32[]{:S(2)}, u32[]{:S(2)}) collective-permute-start(f32[2,256,256]{2,1,0:T(8,128)S(1)} %get-tuple-element.24), channel_id=1, source_target_pairs={{4,12},{12,4},{20,28},{28,20},{36,44},{44,36},{52,60},{60,52},{68,... | collective-permute-start | bytes 1572872 | tf_op jit(solution)/shard_map/ppermute | solution.py:265
  14.7 47.6 %collective-permute-start.1 = (f32[2,512,256]{2,1,0:T(8,128)}, f32[2,512,256]{2,1,0:T(8,128)S(1)}, u32[]{:S(2)}, u32[]{:S(2)}) collective-permute-start(f32[2,512,256]{2,1,0:T(8,128)} %slice.14), channel_id=1, source_target_pairs={{1,0},{2,1},{3,2},{4,3},{5,4},{6,5},{7,6},{9,8},{10,9},{11,10},{12... | collective-permute-start | bytes 3145736 | tf_op jit(solution)/shard_map/ppermute | solution.py:265
  17.9 44.4 %collective-permute-start.2 = (f32[2,512,256]{2,1,0:T(8,128)}, f32[2,512,256]{2,1,0:T(8,128)}, u32[]{:S(2)}, u32[]{:S(2)}) collective-permute-start(f32[2,512,256]{2,1,0:T(8,128)} %collective-permute-done), channel_id=1, source_target_pairs={{7,15},{15,7},{23,31},{31,23},{39,47},{47,39},{55,63},{63,55},{71,... | collective-permute-start | bytes 3145736 | tf_op jit(solution)/shard_map/ppermute | solution.py:265
  19.6 39.3 %collective-permute-start.4 = (f32[2,256,256]{2,1,0:T(8,128)}, f32[2,256,256]{2,1,0:T(8,128)}, u32[]{:S(2)}, u32[]{:S(2)}) collective-permute-start(f32[2,256,256]{2,1,0:T(8,128)} %get-tuple-element.23), channel_id=1, source_target_pairs={{0,12},{1,13},{2,14},{3,15},{4,0},{5,1},{6,2},{7,3},{8,4},{9,5},{1... | collective-permute-start | bytes 1572872 | tf_op jit(solution)/shard_map/ppermute | solution.py:265
  47.7 14.6 %collective-permute-start.5 = (f32[2,256,256]{2,1,0:T(8,128)}, f32[2,256,256]{2,1,0:T(8,128)}, u32[]{:S(2)}, u32[]{:S(2)}) collective-permute-start(f32[2,256,256]{2,1,0:T(8,128)} %collective-permute-done.3.lower_left), channel_id=1, source_target_pairs={{1,0},{2,1},{3,2},{4,3},{5,4},{6,5},{7,6},{9,8},{10,9},{11,10},{12... | collective-permute-start | bytes 1572872 | tf_op jit(solution)/shard_map/ppermute | solution.py:265
  49.6 12.7 %collective-permute-start.7 = (f32[2,256,256]{2,1,0:T(8,128)}, f32[2,256,256]{2,1,0:T(8,128)}, u32[]{:S(2)}, u32[]{:S(2)}) collective-permute-start(f32[2,256,256]{2,1,0:T(8,128)} %collective-permute-done.6), channel_id=1, source_target_pairs={{4,7},{12,15},{20,23},{28,31},{36,39},{44,47},{52,55},{60,63},{68,... | collective-permute-start | bytes 1572872 | tf_op jit(solution)/shard_map/ppermute | solution.py:265
  62.3 1.6 copy-start.1
  63.9 1.0 copy-start.2
  64.9 1.0 copy-start.3
  66.0 1.0 copy-start.4
  83.3 13.8 %collective-permute-start.10 = (f32[2,512,256]{2,1,0:T(8,128)S(1)}, f32[2,512,256]{2,1,0:T(8,128)S(1)}, u32[]{:S(2)}, u32[]{:S(2)}) collective-permute-start(f32[2,512,256]{2,1,0:T(8,128)S(1)} %get-tuple-element.19), channel_id=1, source_target_pairs={{7,0},{15,8},{23,16},{31,24},{39,32},{47,40},{55,48},{63,56},{71,6... | collective-permute-start | bytes 3145736 | tf_op jit(solution)/shard_map/ppermute | solution.py:265
  84.0 8.7 %collective-permute-start.8 = (f32[2,256,256]{2,1,0:T(8,128)S(1)}, f32[2,256,256]{2,1,0:T(8,128)S(1)}, u32[]{:S(2)}, u32[]{:S(2)}) collective-permute-start(f32[2,256,256]{2,1,0:T(8,128)S(1)} %get-tuple-element.17), channel_id=1, source_target_pairs={{0,1},{1,2},{2,3},{3,4},{4,5},{5,6},{6,7},{7,8},{8,9},{9,10},{10,1... | collective-permute-start | bytes 1572872 | tf_op jit(solution)/shard_map/ppermute | solution.py:265
  92.7 56.6 %collective-permute-start.9 = (f32[2,512,256]{2,1,0:T(8,128)S(1)}, f32[2,512,256]{2,1,0:T(8,128)S(1)}, u32[]{:S(2)}, u32[]{:S(2)}) collective-permute-start(f32[2,512,256]{2,1,0:T(8,128)S(1)} %get-tuple-element.19), channel_id=1, source_target_pairs={{0,1},{1,2},{2,3},{3,4},{4,5},{5,6},{6,7},{8,9},{9,10},{10,11},{11... | collective-permute-start | bytes 3145736 | tf_op jit(solution)/shard_map/ppermute | solution.py:265
  97.1 52.2 %collective-permute-start.11 = (f32[2,512,256]{2,1,0:T(8,128)S(1)}, f32[2,512,256]{2,1,0:T(8,128)S(1)}, u32[]{:S(2)}, u32[]{:S(2)}) collective-permute-start(f32[2,512,256]{2,1,0:T(8,128)S(1)} %collective-permute-done.10), channel_id=1, source_target_pairs={{0,8},{8,0},{16,24},{24,16},{32,40},{40,32},{48,56},{56,48},{64,72... | collective-permute-start | bytes 3145736 | tf_op jit(solution)/shard_map/ppermute | solution.py:265
  97.8 40.4 %collective-permute-start.13 = (f32[2,256,256]{2,1,0:T(8,128)S(1)}, f32[2,256,256]{2,1,0:T(8,128)S(1)}, u32[]{:S(2)}, u32[]{:S(2)}) collective-permute-start(f32[2,256,256]{2,1,0:T(8,128)S(1)} %get-tuple-element.22), channel_id=1, source_target_pairs={{0,4},{1,5},{2,6},{3,7},{4,8},{5,9},{6,10},{7,11},{8,12},{9,13},{1... | collective-permute-start | bytes 1572872 | tf_op jit(solution)/shard_map/ppermute | solution.py:265
  105.3 44.0 %collective-permute-start.12 = (f32[2,256,256]{2,1,0:T(8,128)S(1)}, f32[2,256,256]{2,1,0:T(8,128)S(1)}, u32[]{:S(2)}, u32[]{:S(2)}) collective-permute-start(f32[2,256,256]{2,1,0:T(8,128)S(1)} %add.3), channel_id=1, source_target_pairs={{0,4},{1,5},{2,6},{3,7},{4,8},{5,9},{6,10},{7,11},{8,12},{9,13},{1... | collective-permute-start | bytes 1572872 | tf_op jit(solution)/shard_map/ppermute | solution.py:265
  151.0 6.7 %copy-start.5 = (f32[2,16,8]{1,2,0:T(8,128)S(1)}, f32[2,16,8]{1,2,0:T(8,128)}, u32[]{:S(2)}) copy-start(f32[2,16,8]{1,2,0:T(8,128)} %param.11) | copy-start | bytes 3076
  151.0 61.3 %all-to-all-start = ((f32[16,2,32,512]{3,2,1,0:T(8,128)}), f32[16,2,32,512]{3,2,1,0:T(8,128)S(1)}, u32[]{:S(2)}, u32[]{:S(2)}) async-start(f32[16,2,32,512]{3,2,1,0:T(8,128)} %combine.1), calls=%async_computation | async-start | bytes 4194304 | tf_op jit(solution)/shard_map/all_to_all | solution.py:292

commit v4 on v2

--- a/solution.py
+++ b/solution.py
@@ -14,7 +14,7 @@
 FIT_STEPS = 10
 AMPLITUDE_FLOOR = 0.5
 LANES = 128
-GROUP = 4
+GROUP = 8
 VMEM_BYTES = 48 * 2**20
 
 
@@ -45,9 +45,17 @@
 def gradient_kernel(
     corners, own, right, right_far, lower_left, lower_right, corner, corner_far, probe, measured,
     left_table, right_table, main_out, right_out, lower_left_out, lower_right_out, corner_out,
-    field, grad,
+    field, grad, amplitudes, arrived,
 ):
     count, length = measured.shape[0], measured.shape[1]
+    group = math.gcd(GROUP, count)
+
+    def fetch(first):
+        some = pl.ds(first * group, group)
+        return pltpu.make_async_copy(measured.at[some], amplitudes.at[some], arrived.at[first])
+
+    for first in range(count // group):
+        fetch(first).start()
     tile_px = own.shape[1]
     across, beyond = tile_px // LANES, length // LANES
     for part in range(2):
@@ -93,7 +101,7 @@
     def change(number, far):
         far_real, far_imag = far[:, :length], far[:, length:]
         power = jnp.maximum(far_real * far_real + far_imag * far_imag, floor)
-        factor = measured[number].astype(jnp.float32) * (length * lax.rsqrt(power)) - 1.0
+        factor = amplitudes[number].astype(jnp.float32) * (length * lax.rsqrt(power)) - 1.0
         return stack(factor * far_real, factor * far_imag)
 
     def add_terms(number, back):
@@ -115,12 +123,11 @@
                 grad[part, block + i, rows, :] += jnp.where(tail, turned[i], turned[i - 1])
             grad[part, block + beyond, rows, :] += jnp.where(tail, 0.0, turned[beyond - 1])
 
-    group = math.gcd(GROUP, count)
-
     def add_group(first, carry):
         numbers = [first * group + i for i in range(group)]
         waves = [exit_wave(number) for number in numbers]
         far = transforms(waves, left_table[...], right_table[...])
+        fetch(first).wait()
         changes = [change(number, value) for number, value in zip(numbers, far)]
         back = transforms(changes, right_table[...], left_table[...])
         for number, value in zip(numbers, back):
@@ -156,9 +163,15 @@
         out_shape=[
             f32((2, tile_px, tile_px)), f32((2, tile_px, length)), square, square, square,
         ],
-        in_specs=[pl.BlockSpec(memory_space=pltpu.SMEM)] + [vmem] * 11,
+        in_specs=[
+            pl.BlockSpec(memory_space=pltpu.SMEM), *[vmem] * 8,
+            pl.BlockSpec(memory_space=pl.ANY), vmem, vmem,
+        ],
         out_specs=[vmem] * 5,
-        scratch_shapes=[plane, plane],
+        scratch_shapes=[
+            plane, plane, pltpu.VMEM(measured.shape, measured.dtype),
+            pltpu.SemaphoreType.DMA((count // math.gcd(GROUP, count),)),
+        ],
         compiler_params=pltpu.CompilerParams(vmem_limit_bytes=VMEM_BYTES),
         cost_estimate=pl.CostEstimate(
             flops=count * 32 * length**3, bytes_accessed=2**23, transcendentals=0
@@ -170,7 +183,7 @@
 def fit_kernel(spectra, step, rate, data, fitted):
     energies, _, rows, width = data.shape
     materials = step.shape[0]
-    cols = 2 * LANES
+    cols = math.gcd(4 * LANES, width)
     blocks = width // cols
 
     def fit_block(number, carry):
@@ -196,7 +209,7 @@
                 moved.append(jnp.maximum(total, 0.0))
             return tuple(moved)
 
-        coefficients = lax.fori_loop(1, FIT_STEPS, descend, start)
+        coefficients = lax.fori_loop(1, FIT_STEPS, descend, start, unroll=True)
         for part in range(2):
             for energy in range(energies):
                 total = spectra[part, energy * materials] * coefficients[0]
@@ -250,17 +263,22 @@
     main, to_right, to_lower_left, to_lower_right, to_corner = patch_gradients(
         positions[0], own, halos, probe_wave[0], measured[0, 0]
     )
-    beside = move(to_corner, [(t, t + 1) for t in range(tiles)])
-    above_right = move(to_lower_right, [(t, t + TILE_COLS) for t in range(tiles)])
+    beside = move(to_corner, [(t, t + 1) for t in range(tiles) if t % half != last])
+    diagonal = move(to_corner, [(last, 2), (half + last, half + 2)])
     left_step = move(to_right, [(last, 0), (half + last, half)])
+    beside, to_right, to_lower_right = lax.optimization_barrier((beside, to_right, to_lower_right))
+    to_lower = jnp.concatenate([to_lower_left + beside, to_lower_right], 2)
+    above = move(to_lower, [(t, t + TILE_COLS) for t in range(tiles)])
     left = move(to_right, [(t, t + 1) for t in range(tiles) if t % half != last])
+    diagonal = move(diagonal, [(2, half + 2), (half + 2, 2)])
     left_far = move(left_step, [(0, half), (half, 0)])
-    above_left = move(to_lower_left + beside, [(t, t + TILE_COLS) for t in range(tiles)])
-    above = jnp.concatenate([above_left, above_right], 2)
+    diagonal = move(diagonal, [(half + 2, half + TILE_COLS), (2, TILE_COLS)])
+    rest = tile_px - length
     updated = (
         main
-        + jnp.pad(left + left_far, ((0, 0), (0, 0), (0, tile_px - length)))
-        + jnp.pad(above, ((0, 0), (0, tile_px - length), (0, 0)))
+        + jnp.pad(left + left_far, ((0, 0), (0, 0), (0, rest)))
+        + jnp.pad(above, ((0, 0), (0, rest), (0, 0)))
+        + jnp.pad(diagonal, ((0, 0), (0, rest), (0, rest)))
     )
     groups = lax.axis_size("energy")
     outgoing = updated.reshape(2, groups, tile_px // groups, tile_px).transpose(1, 0, 2, 3)

time: 266 us -> 270 us (1.015)
  waiting for transfers between devices: 93.9 us -> 113 us
  starting transfers between devices: 80.9 us -> 65.5 us
    ppermute x14 -> x16, waiting for transfers between devices: 49 us -> 64.7 us  [move(): lax.ppermute(value, 'tile', [(s % tiles, d % tiles) for s, d in pairs])]
    ppermute x14 -> x16, starting transfers between devices: 76.7 us -> 61.2 us  [move(): lax.ppermute(value, 'tile', [(s % tiles, d % tiles) for s, d in pairs])]
    all_to_all x1, waiting for transfers between devices: 44.9 us -> 48.1 us  [body(): lax.all_to_all(outgoing, 'energy', split_axis=0, concat_axis=0, tiled=True)]
  transfers between devices with their start and end apart: 15 -> 17, of which waited for: 6 -> 6; matrix products, arithmetic and copies ran while one was open for 1% -> 1% of each run, Pallas kernels for 0% -> 0%
where the time goes in v4:
time: 270 us; the launch traced here: 266 us
  waiting for transfers between devices  113 us (42%)
  starting transfers between devices  65.5 us (24%)
  blocking collectives  53.5 us (20%)
  Pallas kernels  24 us (9%)
  local copies, waits for them, and re-layouts  7.63 us (3%)
    ppermute x16, waiting for transfers between devices, move(): lax.ppermute(value, 'tile', [(s % tiles, d % tiles) for s, d in pairs])  64.7 us
    ppermute x16, starting transfers between devices, move(): lax.ppermute(value, 'tile', [(s % tiles, d % tiles) for s, d in pairs])  61.2 us
    all_to_all x1, blocking collectives, body(): lax.all_to_all(spectra, 'energy', split_axis=0, concat_axis=0, tiled=True)  53.5 us
    all_to_all x1, waiting for transfers between devices, body(): lax.all_to_all(outgoing, 'energy', split_axis=0, concat_axis=0, tiled=True)  48.1 us
    pallas_call x1, Pallas kernels, patch_gradients(): pl.pallas_call(gradient_kernel, out_shape=[f32((2, tile_px, tile_px)), f3...  18.4 us
    pallas_call x1, Pallas kernels, fit_spectra(): pl.pallas_call(fit_kernel, out_shape=jax.ShapeDtypeStruct(data.shape, jnp...  5.67 us
  transfers between devices with their start and end apart: 17, of which 6 were waited for; matrix products, arithmetic and copies ran while one was open for 1% of the time, Pallas kernels for 0%

profile of v4, /device:TPU:9, one launch (start us, length us, event | category | flops | bytes accessed | tf_op | source)
XLA Modules:
  0.0 266.0 jit_solution(14074653534048272023)
XLA Ops:
  0.0 2.4 slice.14
  2.4 1.7 collective-permute-start.1
  4.1 0.9 fusion
  5.0 8.3 %collective-permute-start.3 = (f32[2,256,256]{2,1,0:T(8,128)S(1)}, f32[2,256,256]{2,1,0:T(8,128)S(1)}, u32[]{:S(2)}, u32[]{:S(2)}) collective-permute-start(f32[2,256,256]{2,1,0:T(8,128)S(1)} %get-tuple-element.22), channel_id=1, source_target_pairs={{0,12},{1,13},{2,14},{3,15},{4,0},{5,1},{6,2},{7,3},{8,4},{9,5},{1... | collective-permute-start | bytes 1572872 | tf_op jit(solution)/shard_map/ppermute | solution.py:249
  13.3 1.4 collective-permute-start.6
  14.7 3.2 %collective-permute-start = (f32[2,512,256]{2,1,0:T(8,128)}, f32[2,512,256]{2,1,0:T(8,128)}, u32[]{:S(2)}, u32[]{:S(2)}) collective-permute-start(f32[2,512,256]{2,1,0:T(8,128)} %slice.14), channel_id=1, source_target_pairs={{1,0},{2,1},{3,2},{4,3},{5,4},{6,5},{7,6},{9,8},{10,9},{11,10},{12... | collective-permute-start | bytes 3145736 | tf_op jit(solution)/shard_map/ppermute | solution.py:249
  17.9 1.7 collective-permute-start.2
  19.6 26.6 %collective-permute-start.4 = (f32[2,256,256]{2,1,0:T(8,128)}, f32[2,256,256]{2,1,0:T(8,128)S(1)}, u32[]{:S(2)}, u32[]{:S(2)}) collective-permute-start(f32[2,256,256]{2,1,0:T(8,128)} %get-tuple-element.21), channel_id=1, source_target_pairs={{0,12},{1,13},{2,14},{3,15},{4,0},{5,1},{6,2},{7,3},{8,4},{9,5},{1... | collective-permute-start | bytes 1572872 | tf_op jit(solution)/shard_map/ppermute | solution.py:249
  46.2 1.9 collective-permute-start.5
  48.2 0.7 collective-permute-start.7
  49.0 9.9 %collective-permute-done.4.lower_right = f32[2,256,256]{2,1,0:T(8,128)S(1)} collective-permute-done((f32[2,256,256]{2,1,0:T(8,128)}, f32[2,256,256]{2,1,0:T(8,128)S(1)}, u32[]{:S(2)}, u32[]{:S(2)}) %collective-permute-start.4) | collective-permute-done | bytes 524320 | tf_op jit(solution)/shard_map/ppermute | solution.py:249
  58.9 1.0 copy-done.2
  60.0 18.4 %patch_gradients.1 = (f32[2,512,512]{2,1,0:T(8,128)}, f32[2,512,256]{2,1,0:T(8,128)}, f32[2,256,256]{2,1,0:T(8,128)S(1)}, f32[2,256,256]{2,1,0:T(8,128)S(1)}, f32[2,256,256]{2,1,0:T(8,128)S(1)}) custom-call(s32[16,2]{1,0:T(8,128)S(1)} %copy.11.corners, f32[2,512,512]{2,1,0:T(8,128)} %bitcast.22, f32[2,512,256]{2,1,0:T(8,128)} %collective-permute-done.right, ...), custom_call_target="tpu_custom_call" | custom-call | flops 8589934592 | bytes 8388608 | tf_op jit(solution)/shard_map/patch_gradients/pallas_call | solution.py:161
  78.3 0.7 collective-permute-start.10
  79.1 6.9 %collective-permute-start.8 = (f32[2,256,256]{2,1,0:T(8,128)S(1)}, f32[2,256,256]{2,1,0:T(8,128)S(1)}, u32[]{:S(2)}, u32[]{:S(2)}) collective-permute-start(f32[2,256,256]{2,1,0:T(8,128)S(1)} %get-tuple-element.14), channel_id=1, source_target_pairs={{0,1},{1,2},{2,3},{3,4},{4,5},{5,6},{6,7},{8,9},{9,10},{10,11},{11... | collective-permute-start | bytes 1572872 | tf_op jit(solution)/shard_map/ppermute | solution.py:249
  86.0 0.7 collective-permute-start.13
  86.7 5.4 %collective-permute-done.8 = f32[2,256,256]{2,1,0:T(8,128)S(1)} collective-permute-done((f32[2,256,256]{2,1,0:T(8,128)S(1)}, f32[2,256,256]{2,1,0:T(8,128)S(1)}, u32[]{:S(2)}, u32[]{:S(2)}) %collective-permute-start.8) | collective-permute-done | bytes 524320 | tf_op jit(solution)/shard_map/ppermute | solution.py:249
  92.1 4.4 %collective-permute-start.9 = (f32[2,512,256]{2,1,0:T(8,128)}, f32[2,512,256]{2,1,0:T(8,128)S(1)}, u32[]{:S(2)}, u32[]{:S(2)}) collective-permute-start(f32[2,512,256]{2,1,0:T(8,128)} %get-tuple-element.17), channel_id=1, source_target_pairs={{0,1},{1,2},{2,3},{3,4},{4,5},{5,6},{6,7},{8,9},{9,10},{10,11},{11... | collective-permute-start | bytes 3145736 | tf_op jit(solution)/shard_map/ppermute | solution.py:249
  96.7 0.9 collective-permute-start.11
  97.6 0.7 collective-permute-start.14
  98.3 0.7 collective-permute-start.12
  98.9 0.9 collective-permute-start.15
  99.8 35.7 %collective-permute-done.9 = f32[2,512,256]{2,1,0:T(8,128)S(1)} collective-permute-done((f32[2,512,256]{2,1,0:T(8,128)}, f32[2,512,256]{2,1,0:T(8,128)S(1)}, u32[]{:S(2)}, u32[]{:S(2)}) %collective-permute-start.9) | collective-permute-done | bytes 1048608 | tf_op jit(solution)/shard_map/ppermute | solution.py:249
  135.6 13.6 %collective-permute-done.12 = f32[2,256,512]{2,1,0:T(8,128)S(1)} collective-permute-done((f32[2,256,512]{2,1,0:T(8,128)S(1)}, f32[2,256,512]{2,1,0:T(8,128)S(1)}, u32[]{:S(2)}, u32[]{:S(2)}) %collective-permute-start.12) | collective-permute-done | bytes 1048608 | tf_op jit(solution)/shard_map/ppermute | solution.py:249
  149.2 0.5 pad_add_fusion
  149.7 1.5 copy.16
  151.2 4.2 %all-to-all-start = ((f32[16,2,32,512]{3,2,1,0:T(8,128)}), f32[16,2,32,512]{3,2,1,0:T(8,128)S(1)}, u32[]{:S(2)}, u32[]{:S(2)}) async-start(f32[16,2,32,512]{3,2,1,0:T(8,128)} %bitcast.18), calls=%async_computation | async-start | bytes 4194304 | tf_op jit(solution)/shard_map/all_to_all | solution.py:285
  155.6 0.8 select_reduce_fusion
  157.2 48.1 %all-to-all-done.data = f32[16,2,32,512]{3,2,1,0:T(8,128)S(1)} async-done(((f32[16,2,32,512]{3,2,1,0:T(8,128)}), f32[16,2,32,512]{3,2,1,0:T(8,128)S(1)}, u32[]{:S(2)}, u32[]{:S(2)}) %all-to-all-start) | async-done | bytes 2097184 | tf_op jit(solution)/shard_map/all_to_all | solution.py:285
  205.3 5.7 %fit_spectra.1 = f32[16,2,32,512]{3,2,1,0:T(8,128)S(1)} custom-call(f32[2,128]{1,0:T(2,128)S(1)} %reshape.12.spectra, f32[8,8]{1,0:T(8,128)S(1)} %multiply_subtract_fusion.step, f32[1]{0:T(128)} %bitcast.1.rate, f32[16,2,32,512]{3,2,1,0:T(8,128)S(1)} %all-to-all-done.data), custom_call_target="tpu_custom_call" | custom-call | tf_op jit(solution)/shard_map/fit_spectra/pallas_call | solution.py:230
  211.0 53.5 %all_to_all.10 = f32[16,2,32,512]{3,2,1,0:T(8,128)S(1)} all-to-all(f32[16,2,32,512]{3,2,1,0:T(8,128)S(1)} %fit_spectra.1), channel_id=1, replica_groups=mesh['energy'=16,'tile'=16] {'energy'}, dimensions={0} | all-to-all | bytes 4194304 | tf_op jit(solution)/shard_map/all_to_all | solution.py:287
  264.5 1.5 copy.13
  (32 shorter events, 0.7 us)
Async XLA Ops:
  0.0 4.1 %copy-start.3 = (f32[1,2,1,512,512]{4,3,2,1,0:T(8,128)S(1)}, f32[1,2,1,512,512]{4,3,2,1,0:T(8,128)}, u32[]{:S(2)}) copy-start(f32[1,2,1,512,512]{4,3,2,1,0:T(8,128)} %param.7) | copy-start | bytes 6291460
  0.0 48.9 %copy-start.6 = (s32[1,16,2]{1,2,0:T(2,128)S(1)}, s32[1,16,2]{1,2,0:T(2,128)}, u32[]{:S(2)}) copy-start(s32[1,16,2]{1,2,0:T(2,128)} %param.10) | copy-start | bytes 388
  0.0 58.9 %copy-start = (f32[1,2,256,256]{3,2,1,0:T(8,128)S(1)}, f32[1,2,256,256]{3,2,1,0:T(8,128)}, u32[]{:S(2)}) copy-start(f32[1,2,256,256]{3,2,1,0:T(8,128)} %param.8) | copy-start | bytes 1572868
  0.0 58.9 %copy-start.1 = (bf16[512,512]{1,0:T(8,128)(2,1)S(1)}, bf16[512,512]{1,0:T(8,128)(2,1)}, u32[]{:S(2)}) copy-start(bf16[512,512]{1,0:T(8,128)(2,1)} %constant.13.clone.left_table) | copy-start | bytes 1572868
  2.4 15.5 %collective-permute-start.1 = (f32[2,512,256]{2,1,0:T(8,128)}, f32[2,512,256]{2,1,0:T(8,128)}, u32[]{:S(2)}, u32[]{:S(2)}) collective-permute-start(f32[2,512,256]{2,1,0:T(8,128)} %slice.14), channel_id=1, source_target_pairs={{0,7},{8,15},{16,23},{24,31},{32,39},{40,47},{48,55},{56,63},{64,7... | collective-permute-start | bytes 3145736 | tf_op jit(solution)/shard_map/ppermute | solution.py:249
  5.0 41.2 %collective-permute-start.3 = (f32[2,256,256]{2,1,0:T(8,128)S(1)}, f32[2,256,256]{2,1,0:T(8,128)S(1)}, u32[]{:S(2)}, u32[]{:S(2)}) collective-permute-start(f32[2,256,256]{2,1,0:T(8,128)S(1)} %get-tuple-element.22), channel_id=1, source_target_pairs={{0,12},{1,13},{2,14},{3,15},{4,0},{5,1},{6,2},{7,3},{8,4},{9,5},{1... | collective-permute-start | bytes 1572872 | tf_op jit(solution)/shard_map/ppermute | solution.py:249
  13.3 34.9 %collective-permute-start.6 = (f32[2,256,256]{2,1,0:T(8,128)S(1)}, f32[2,256,256]{2,1,0:T(8,128)}, u32[]{:S(2)}, u32[]{:S(2)}) collective-permute-start(f32[2,256,256]{2,1,0:T(8,128)S(1)} %get-tuple-element.22), channel_id=1, source_target_pairs={{4,12},{12,4},{20,28},{28,20},{36,44},{44,36},{52,60},{60,52},{68,... | collective-permute-start | bytes 1572872 | tf_op jit(solution)/shard_map/ppermute | solution.py:249
  14.7 44.2 %collective-permute-start = (f32[2,512,256]{2,1,0:T(8,128)}, f32[2,512,256]{2,1,0:T(8,128)}, u32[]{:S(2)}, u32[]{:S(2)}) collective-permute-start(f32[2,512,256]{2,1,0:T(8,128)} %slice.14), channel_id=1, source_target_pairs={{1,0},{2,1},{3,2},{4,3},{5,4},{6,5},{7,6},{9,8},{10,9},{11,10},{12... | collective-permute-start | bytes 3145736 | tf_op jit(solution)/shard_map/ppermute | solution.py:249
  17.9 41.0 %collective-permute-start.2 = (f32[2,512,256]{2,1,0:T(8,128)}, f32[2,512,256]{2,1,0:T(8,128)}, u32[]{:S(2)}, u32[]{:S(2)}) collective-permute-start(f32[2,512,256]{2,1,0:T(8,128)} %collective-permute-done.1), channel_id=1, source_target_pairs={{7,15},{15,7},{23,31},{31,23},{39,47},{47,39},{55,63},{63,55},{71,... | collective-permute-start | bytes 3145736 | tf_op jit(solution)/shard_map/ppermute | solution.py:249
  19.6 39.2 %collective-permute-start.4 = (f32[2,256,256]{2,1,0:T(8,128)}, f32[2,256,256]{2,1,0:T(8,128)S(1)}, u32[]{:S(2)}, u32[]{:S(2)}) collective-permute-start(f32[2,256,256]{2,1,0:T(8,128)} %get-tuple-element.21), channel_id=1, source_target_pairs={{0,12},{1,13},{2,14},{3,15},{4,0},{5,1},{6,2},{7,3},{8,4},{9,5},{1... | collective-permute-start | bytes 1572872 | tf_op jit(solution)/shard_map/ppermute | solution.py:249
  46.2 12.7 %collective-permute-start.5 = (f32[2,256,256]{2,1,0:T(8,128)S(1)}, f32[2,256,256]{2,1,0:T(8,128)S(1)}, u32[]{:S(2)}, u32[]{:S(2)}) collective-permute-start(f32[2,256,256]{2,1,0:T(8,128)S(1)} %collective-permute-done.3.lower_left), channel_id=1, source_target_pairs={{1,0},{2,1},{3,2},{4,3},{5,4},{6,5},{7,6},{9,8},{10,9},{11,10},{12... | collective-permute-start | bytes 1572872 | tf_op jit(solution)/shard_map/ppermute | solution.py:249
  48.2 10.7 %collective-permute-start.7 = (f32[2,256,256]{2,1,0:T(8,128)}, f32[2,256,256]{2,1,0:T(8,128)S(1)}, u32[]{:S(2)}, u32[]{:S(2)}) collective-permute-start(f32[2,256,256]{2,1,0:T(8,128)} %collective-permute-done.6), channel_id=1, source_target_pairs={{4,7},{12,15},{20,23},{28,31},{36,39},{44,47},{52,55},{60,63},{68,... | collective-permute-start | bytes 1572872 | tf_op jit(solution)/shard_map/ppermute | solution.py:249
  58.9 1.0 copy-start.2
  78.3 18.4 %collective-permute-start.10 = (f32[2,512,256]{2,1,0:T(8,128)}, f32[2,512,256]{2,1,0:T(8,128)S(1)}, u32[]{:S(2)}, u32[]{:S(2)}) collective-permute-start(f32[2,512,256]{2,1,0:T(8,128)} %get-tuple-element.17), channel_id=1, source_target_pairs={{7,0},{15,8},{23,16},{31,24},{39,32},{47,40},{55,48},{63,56},{71,6... | collective-permute-start | bytes 3145736 | tf_op jit(solution)/shard_map/ppermute | solution.py:249
  79.1 13.0 %collective-permute-start.8 = (f32[2,256,256]{2,1,0:T(8,128)S(1)}, f32[2,256,256]{2,1,0:T(8,128)S(1)}, u32[]{:S(2)}, u32[]{:S(2)}) collective-permute-start(f32[2,256,256]{2,1,0:T(8,128)S(1)} %get-tuple-element.14), channel_id=1, source_target_pairs={{0,1},{1,2},{2,3},{3,4},{4,5},{5,6},{6,7},{8,9},{9,10},{10,11},{11... | collective-permute-start | bytes 1572872 | tf_op jit(solution)/shard_map/ppermute | solution.py:249
  86.0 11.6 %collective-permute-start.13 = (f32[2,256,256]{2,1,0:T(8,128)S(1)}, f32[2,256,256]{2,1,0:T(8,128)S(1)}, u32[]{:S(2)}, u32[]{:S(2)}) collective-permute-start(f32[2,256,256]{2,1,0:T(8,128)S(1)} %get-tuple-element.14), channel_id=1, source_target_pairs={{7,2},{15,10},{23,18},{31,26},{39,34},{47,42},{55,50},{63,58},{71,... | collective-permute-start | bytes 1572872 | tf_op jit(solution)/shard_map/ppermute | solution.py:249
  92.1 43.4 %collective-permute-start.9 = (f32[2,512,256]{2,1,0:T(8,128)}, f32[2,512,256]{2,1,0:T(8,128)S(1)}, u32[]{:S(2)}, u32[]{:S(2)}) collective-permute-start(f32[2,512,256]{2,1,0:T(8,128)} %get-tuple-element.17), channel_id=1, source_target_pairs={{0,1},{1,2},{2,3},{3,4},{4,5},{5,6},{6,7},{8,9},{9,10},{10,11},{11... | collective-permute-start | bytes 3145736 | tf_op jit(solution)/shard_map/ppermute | solution.py:249
  96.7 52.6 %copy-start.4 = (f32[2,512,512]{2,1,0:T(8,128)S(1)}, f32[2,512,512]{2,1,0:T(8,128)}, u32[]{:S(2)}) copy-start(f32[2,512,512]{2,1,0:T(8,128)} %get-tuple-element.13) | copy-start | bytes 6291460
  96.7 38.8 %collective-permute-start.11 = (f32[2,512,256]{2,1,0:T(8,128)S(1)}, f32[2,512,256]{2,1,0:T(8,128)S(1)}, u32[]{:S(2)}, u32[]{:S(2)}) collective-permute-start(f32[2,512,256]{2,1,0:T(8,128)S(1)} %collective-permute-done.10), channel_id=1, source_target_pairs={{0,8},{8,0},{16,24},{24,16},{32,40},{40,32},{48,56},{56,48},{64,72... | collective-permute-start | bytes 3145736 | tf_op jit(solution)/shard_map/ppermute | solution.py:249
  97.6 1.4 collective-permute-start.14
  98.3 51.0 %collective-permute-start.12 = (f32[2,256,512]{2,1,0:T(8,128)S(1)}, f32[2,256,512]{2,1,0:T(8,128)S(1)}, u32[]{:S(2)}, u32[]{:S(2)}) collective-permute-start(f32[2,256,512]{2,1,0:T(8,128)S(1)} %pad_maximum_fusion), channel_id=1, source_target_pairs={{0,4},{1,5},{2,6},{3,7},{4,8},{5,9},{6,10},{7,11},{8,12},{9,13},{1... | collective-permute-start | bytes 3145736 | tf_op jit(solution)/shard_map/ppermute | solution.py:249
  98.9 50.3 %collective-permute-start.15 = (f32[2,256,256]{2,1,0:T(8,128)S(1)}, f32[2,256,256]{2,1,0:T(8,128)S(1)}, u32[]{:S(2)}, u32[]{:S(2)}) collective-permute-start(f32[2,256,256]{2,1,0:T(8,128)S(1)} %collective-permute-done.14), channel_id=1, source_target_pairs={{10,12},{2,4},{26,28},{18,20},{42,44},{34,36},{58,60},{50,52},{74,... | collective-permute-start | bytes 1572872 | tf_op jit(solution)/shard_map/ppermute | solution.py:249
  151.2 4.2 %copy-start.5 = (f32[2,16,8]{1,2,0:T(8,128)S(1)}, f32[2,16,8]{1,2,0:T(8,128)}, u32[]{:S(2)}) copy-start(f32[2,16,8]{1,2,0:T(8,128)} %param.11) | copy-start | bytes 3076
  151.2 54.1 %all-to-all-start = ((f32[16,2,32,512]{3,2,1,0:T(8,128)}), f32[16,2,32,512]{3,2,1,0:T(8,128)S(1)}, u32[]{:S(2)}, u32[]{:S(2)}) async-start(f32[16,2,32,512]{3,2,1,0:T(8,128)} %bitcast.18), calls=%async_computation | async-start | bytes 4194304 | tf_op jit(solution)/shard_map/all_to_all | solution.py:285

commit v5 on v4

--- a/solution.py
+++ b/solution.py
@@ -263,22 +263,17 @@
     main, to_right, to_lower_left, to_lower_right, to_corner = patch_gradients(
         positions[0], own, halos, probe_wave[0], measured[0, 0]
     )
-    beside = move(to_corner, [(t, t + 1) for t in range(tiles) if t % half != last])
-    diagonal = move(to_corner, [(last, 2), (half + last, half + 2)])
+    beside = move(to_corner, [(t, t + 1) for t in range(tiles)])
+    above_right = move(to_lower_right, [(t, t + TILE_COLS) for t in range(tiles)])
     left_step = move(to_right, [(last, 0), (half + last, half)])
-    beside, to_right, to_lower_right = lax.optimization_barrier((beside, to_right, to_lower_right))
-    to_lower = jnp.concatenate([to_lower_left + beside, to_lower_right], 2)
-    above = move(to_lower, [(t, t + TILE_COLS) for t in range(tiles)])
     left = move(to_right, [(t, t + 1) for t in range(tiles) if t % half != last])
-    diagonal = move(diagonal, [(2, half + 2), (half + 2, 2)])
     left_far = move(left_step, [(0, half), (half, 0)])
-    diagonal = move(diagonal, [(half + 2, half + TILE_COLS), (2, TILE_COLS)])
-    rest = tile_px - length
+    above_left = move(to_lower_left + beside, [(t, t + TILE_COLS) for t in range(tiles)])
+    above = jnp.concatenate([above_left, above_right], 2)
     updated = (
         main
-        + jnp.pad(left + left_far, ((0, 0), (0, 0), (0, rest)))
-        + jnp.pad(above, ((0, 0), (0, rest), (0, 0)))
-        + jnp.pad(diagonal, ((0, 0), (0, rest), (0, rest)))
+        + jnp.pad(left + left_far, ((0, 0), (0, 0), (0, tile_px - length)))
+        + jnp.pad(above, ((0, 0), (0, tile_px - length), (0, 0)))
     )
     groups = lax.axis_size("energy")
     outgoing = updated.reshape(2, groups, tile_px // groups, tile_px).transpose(1, 0, 2, 3)

time: 270 us -> 263 us (0.974)
  waiting for transfers between devices: 113 us -> 93.7 us
  starting transfers between devices: 65.5 us -> 81 us
    ppermute x16 -> x14, waiting for transfers between devices: 64.7 us -> 48.8 us  [move(): lax.ppermute(value, 'tile', [(s % tiles, d % tiles) for s, d in pairs])]
    ppermute x16 -> x14, starting transfers between devices: 61.2 us -> 76.8 us  [move(): lax.ppermute(value, 'tile', [(s % tiles, d % tiles) for s, d in pairs])]
    all_to_all x1, waiting for transfers between devices: 48.1 us -> 44.9 us  [body(): lax.all_to_all(outgoing, 'energy', split_axis=0, concat_axis=0, tiled=True)]
  transfers between devices with their start and end apart: 17 -> 15, of which waited for: 6 -> 6; matrix products, arithmetic and copies ran while one was open for 1% -> 1% of each run, Pallas kernels for 0% -> 0%
where the time goes in v5:
time: 263 us; the launch traced here: 261 us
  waiting for transfers between devices  93.7 us (36%)
  starting transfers between devices  81 us (31%)
  blocking collectives  52.5 us (20%)
  Pallas kernels  24.1 us (9%)
  local copies, waits for them, and re-layouts  7.62 us (3%)
    ppermute x14, starting transfers between devices, move(): lax.ppermute(value, 'tile', [(s % tiles, d % tiles) for s, d in pairs])  76.8 us
    all_to_all x1, blocking collectives, body(): lax.all_to_all(spectra, 'energy', split_axis=0, concat_axis=0, tiled=True)  52.5 us
    ppermute x14, waiting for transfers between devices, move(): lax.ppermute(value, 'tile', [(s % tiles, d % tiles) for s, d in pairs])  48.8 us
    all_to_all x1, waiting for transfers between devices, body(): lax.all_to_all(outgoing, 'energy', split_axis=0, concat_axis=0, tiled=True)  44.9 us
    pallas_call x1, Pallas kernels, patch_gradients(): pl.pallas_call(gradient_kernel, out_shape=[f32((2, tile_px, tile_px)), f3...  18.4 us
    pallas_call x1, Pallas kernels, fit_spectra(): pl.pallas_call(fit_kernel, out_shape=jax.ShapeDtypeStruct(data.shape, jnp...  5.67 us
  transfers between devices with their start and end apart: 15, of which 6 were waited for; matrix products, arithmetic and copies ran while one was open for 1% of the time, Pallas kernels for 0%

profile of v5, /device:TPU:9, one launch (start us, length us, event | category | flops | bytes accessed | tf_op | source)
XLA Modules:
  0.0 261.2 jit_solution(17015994568365675398)
XLA Ops:
  0.0 2.4 slice.14
  2.4 1.7 collective-permute-start.1
  4.1 0.9 fusion.1
  5.0 8.3 %collective-permute-start.3 = (f32[2,256,256]{2,1,0:T(8,128)S(1)}, f32[2,256,256]{2,1,0:T(8,128)S(1)}, u32[]{:S(2)}, u32[]{:S(2)}) collective-permute-start(f32[2,256,256]{2,1,0:T(8,128)S(1)} %get-tuple-element.16), channel_id=1, source_target_pairs={{0,12},{1,13},{2,14},{3,15},{4,0},{5,1},{6,2},{7,3},{8,4},{9,5},{1... | collective-permute-start | bytes 1572872 | tf_op jit(solution)/shard_map/ppermute | solution.py:249
  13.3 1.4 collective-permute-start.6
  14.7 3.2 %collective-permute-start = (f32[2,512,256]{2,1,0:T(8,128)}, f32[2,512,256]{2,1,0:T(8,128)}, u32[]{:S(2)}, u32[]{:S(2)}) collective-permute-start(f32[2,512,256]{2,1,0:T(8,128)} %slice.14), channel_id=1, source_target_pairs={{1,0},{2,1},{3,2},{4,3},{5,4},{6,5},{7,6},{9,8},{10,9},{11,10},{12... | collective-permute-start | bytes 3145736 | tf_op jit(solution)/shard_map/ppermute | solution.py:249
  17.9 1.6 collective-permute-start.2
  19.6 26.6 %collective-permute-start.4 = (f32[2,256,256]{2,1,0:T(8,128)}, f32[2,256,256]{2,1,0:T(8,128)S(1)}, u32[]{:S(2)}, u32[]{:S(2)}) collective-permute-start(f32[2,256,256]{2,1,0:T(8,128)} %get-tuple-element.15), channel_id=1, source_target_pairs={{0,12},{1,13},{2,14},{3,15},{4,0},{5,1},{6,2},{7,3},{8,4},{9,5},{1... | collective-permute-start | bytes 1572872 | tf_op jit(solution)/shard_map/ppermute | solution.py:249
  46.2 1.9 collective-permute-start.5
  48.1 0.7 collective-permute-start.7
  48.9 9.9 %collective-permute-done.4.lower_right = f32[2,256,256]{2,1,0:T(8,128)S(1)} collective-permute-done((f32[2,256,256]{2,1,0:T(8,128)}, f32[2,256,256]{2,1,0:T(8,128)S(1)}, u32[]{:S(2)}, u32[]{:S(2)}) %collective-permute-start.4) | collective-permute-done | bytes 524320 | tf_op jit(solution)/shard_map/ppermute | solution.py:249
  58.9 1.0 copy-done.2
  60.0 18.4 %patch_gradients.1 = (f32[2,512,512]{2,1,0:T(8,128)}, f32[2,512,256]{2,1,0:T(8,128)}, f32[2,256,256]{2,1,0:T(8,128)S(1)}, f32[2,256,256]{2,1,0:T(8,128)S(1)}, f32[2,256,256]{2,1,0:T(8,128)S(1)}) custom-call(s32[16,2]{1,0:T(8,128)S(1)} %copy.11.corners, f32[2,512,512]{2,1,0:T(8,128)} %bitcast.22, f32[2,512,256]{2,1,0:T(8,128)} %collective-permute-done.right, ...), custom_call_target="tpu_custom_call" | custom-call | flops 8589934592 | bytes 8388608 | tf_op jit(solution)/shard_map/patch_gradients/pallas_call | solution.py:161
  78.4 0.7 collective-permute-start.9
  79.1 6.8 %collective-permute-start.8 = (f32[2,512,256]{2,1,0:T(8,128)}, f32[2,512,256]{2,1,0:T(8,128)S(1)}, u32[]{:S(2)}, u32[]{:S(2)}) collective-permute-start(f32[2,512,256]{2,1,0:T(8,128)} %get-tuple-element.11), channel_id=1, source_target_pairs={{0,1},{1,2},{2,3},{3,4},{4,5},{5,6},{6,7},{8,9},{9,10},{10,11},{11... | collective-permute-start | bytes 3145736 | tf_op jit(solution)/shard_map/ppermute | solution.py:249
  85.9 0.1 collective-permute-start.11
  86.0 0.7 collective-permute-start.10
  86.7 22.7 %collective-permute-start.13 = (f32[2,256,256]{2,1,0:T(8,128)S(1)}, f32[2,256,256]{2,1,0:T(8,128)S(1)}, u32[]{:S(2)}, u32[]{:S(2)}) collective-permute-start(f32[2,256,256]{2,1,0:T(8,128)S(1)} %get-tuple-element.14), channel_id=1, source_target_pairs={{0,4},{1,5},{2,6},{3,7},{4,8},{5,9},{6,10},{7,11},{8,12},{9,13},{1... | collective-permute-start | bytes 1572872 | tf_op jit(solution)/shard_map/ppermute | solution.py:249
  109.4 5.2 %collective-permute-done.11 = f32[2,256,256]{2,1,0:T(8,128)S(1)} collective-permute-done((f32[2,256,256]{2,1,0:T(8,128)S(1)}, f32[2,256,256]{2,1,0:T(8,128)S(1)}, u32[]{:S(2)}, u32[]{:S(2)}) %collective-permute-start.11) | collective-permute-done | bytes 524320 | tf_op jit(solution)/shard_map/ppermute | solution.py:249
  114.8 0.3 collective-permute-start.12
  115.0 0.1 add.16
  115.2 28.2 %collective-permute-done.13 = f32[2,256,256]{2,1,0:T(8,128)S(1)} collective-permute-done((f32[2,256,256]{2,1,0:T(8,128)S(1)}, f32[2,256,256]{2,1,0:T(8,128)S(1)}, u32[]{:S(2)}, u32[]{:S(2)}) %collective-permute-start.13) | collective-permute-done | bytes 524320 | tf_op jit(solution)/shard_map/ppermute | solution.py:249
  143.4 5.4 %collective-permute-done.12 = f32[2,256,256]{2,1,0:T(8,128)S(1)} collective-permute-done((f32[2,256,256]{2,1,0:T(8,128)S(1)}, f32[2,256,256]{2,1,0:T(8,128)S(1)}, u32[]{:S(2)}, u32[]{:S(2)}) %collective-permute-start.12) | collective-permute-done | bytes 524320 | tf_op jit(solution)/shard_map/ppermute | solution.py:249
  148.8 0.4 fusion
  149.2 1.5 copy.16
  150.7 4.2 %all-to-all-start = ((f32[16,2,32,512]{3,2,1,0:T(8,128)}), f32[16,2,32,512]{3,2,1,0:T(8,128)S(1)}, u32[]{:S(2)}, u32[]{:S(2)}) async-start(f32[16,2,32,512]{3,2,1,0:T(8,128)} %bitcast.19), calls=%async_computation | async-start | bytes 4194304 | tf_op jit(solution)/shard_map/all_to_all | solution.py:280
  155.0 0.1 reshape.12.spectra
  155.1 0.8 select_reduce_fusion
  156.6 44.9 %all-to-all-done.data = f32[16,2,32,512]{3,2,1,0:T(8,128)S(1)} async-done(((f32[16,2,32,512]{3,2,1,0:T(8,128)}), f32[16,2,32,512]{3,2,1,0:T(8,128)S(1)}, u32[]{:S(2)}, u32[]{:S(2)}) %all-to-all-start) | async-done | bytes 2097184 | tf_op jit(solution)/shard_map/all_to_all | solution.py:280
  201.5 5.7 %fit_spectra.1 = f32[16,2,32,512]{3,2,1,0:T(8,128)S(1)} custom-call(f32[2,128]{1,0:T(2,128)S(1)} %reshape.12.spectra, f32[8,8]{1,0:T(8,128)S(1)} %multiply_subtract_fusion.step, f32[1]{0:T(128)} %bitcast.1.rate, f32[16,2,32,512]{3,2,1,0:T(8,128)S(1)} %all-to-all-done.data), custom_call_target="tpu_custom_call" | custom-call | tf_op jit(solution)/shard_map/fit_spectra/pallas_call | solution.py:230
  207.2 52.5 %all_to_all.10 = f32[16,2,32,512]{3,2,1,0:T(8,128)S(1)} all-to-all(f32[16,2,32,512]{3,2,1,0:T(8,128)S(1)} %fit_spectra.1), channel_id=1, replica_groups=mesh['energy'=16,'tile'=16] {'energy'}, dimensions={0} | all-to-all | bytes 4194304 | tf_op jit(solution)/shard_map/all_to_all | solution.py:282
  259.7 1.5 copy.13
  (27 shorter events, 0.3 us)
Async XLA Ops:
  0.0 4.1 %copy-start.4 = (f32[1,2,1,512,512]{4,3,2,1,0:T(8,128)S(1)}, f32[1,2,1,512,512]{4,3,2,1,0:T(8,128)}, u32[]{:S(2)}) copy-start(f32[1,2,1,512,512]{4,3,2,1,0:T(8,128)} %param.7) | copy-start | bytes 6291460
  0.0 48.8 %copy-start.6 = (s32[1,16,2]{1,2,0:T(2,128)S(1)}, s32[1,16,2]{1,2,0:T(2,128)}, u32[]{:S(2)}) copy-start(s32[1,16,2]{1,2,0:T(2,128)} %param.10) | copy-start | bytes 388
  0.0 58.9 %copy-start = (f32[1,2,256,256]{3,2,1,0:T(8,128)S(1)}, f32[1,2,256,256]{3,2,1,0:T(8,128)}, u32[]{:S(2)}) copy-start(f32[1,2,256,256]{3,2,1,0:T(8,128)} %param.8) | copy-start | bytes 1572868
  0.0 58.9 %copy-start.1 = (bf16[512,512]{1,0:T(8,128)(2,1)S(1)}, bf16[512,512]{1,0:T(8,128)(2,1)}, u32[]{:S(2)}) copy-start(bf16[512,512]{1,0:T(8,128)(2,1)} %constant.13.clone.left_table) | copy-start | bytes 1572868
  2.4 15.5 %collective-permute-start.1 = (f32[2,512,256]{2,1,0:T(8,128)}, f32[2,512,256]{2,1,0:T(8,128)}, u32[]{:S(2)}, u32[]{:S(2)}) collective-permute-start(f32[2,512,256]{2,1,0:T(8,128)} %slice.14), channel_id=1, source_target_pairs={{0,7},{8,15},{16,23},{24,31},{32,39},{40,47},{48,55},{56,63},{64,7... | collective-permute-start | bytes 3145736 | tf_op jit(solution)/shard_map/ppermute | solution.py:249
  5.0 41.2 %collective-permute-start.3 = (f32[2,256,256]{2,1,0:T(8,128)S(1)}, f32[2,256,256]{2,1,0:T(8,128)S(1)}, u32[]{:S(2)}, u32[]{:S(2)}) collective-permute-start(f32[2,256,256]{2,1,0:T(8,128)S(1)} %get-tuple-element.16), channel_id=1, source_target_pairs={{0,12},{1,13},{2,14},{3,15},{4,0},{5,1},{6,2},{7,3},{8,4},{9,5},{1... | collective-permute-start | bytes 1572872 | tf_op jit(solution)/shard_map/ppermute | solution.py:249
  13.3 34.9 %collective-permute-start.6 = (f32[2,256,256]{2,1,0:T(8,128)S(1)}, f32[2,256,256]{2,1,0:T(8,128)}, u32[]{:S(2)}, u32[]{:S(2)}) collective-permute-start(f32[2,256,256]{2,1,0:T(8,128)S(1)} %get-tuple-element.16), channel_id=1, source_target_pairs={{4,12},{12,4},{20,28},{28,20},{36,44},{44,36},{52,60},{60,52},{68,... | collective-permute-start | bytes 1572872 | tf_op jit(solution)/shard_map/ppermute | solution.py:249
  14.7 44.2 %collective-permute-start = (f32[2,512,256]{2,1,0:T(8,128)}, f32[2,512,256]{2,1,0:T(8,128)}, u32[]{:S(2)}, u32[]{:S(2)}) collective-permute-start(f32[2,512,256]{2,1,0:T(8,128)} %slice.14), channel_id=1, source_target_pairs={{1,0},{2,1},{3,2},{4,3},{5,4},{6,5},{7,6},{9,8},{10,9},{11,10},{12... | collective-permute-start | bytes 3145736 | tf_op jit(solution)/shard_map/ppermute | solution.py:249
  17.9 41.0 %collective-permute-start.2 = (f32[2,512,256]{2,1,0:T(8,128)}, f32[2,512,256]{2,1,0:T(8,128)}, u32[]{:S(2)}, u32[]{:S(2)}) collective-permute-start(f32[2,512,256]{2,1,0:T(8,128)} %collective-permute-done.1), channel_id=1, source_target_pairs={{7,15},{15,7},{23,31},{31,23},{39,47},{47,39},{55,63},{63,55},{71,... | collective-permute-start | bytes 3145736 | tf_op jit(solution)/shard_map/ppermute | solution.py:249
  19.6 39.2 %collective-permute-start.4 = (f32[2,256,256]{2,1,0:T(8,128)}, f32[2,256,256]{2,1,0:T(8,128)S(1)}, u32[]{:S(2)}, u32[]{:S(2)}) collective-permute-start(f32[2,256,256]{2,1,0:T(8,128)} %get-tuple-element.15), channel_id=1, source_target_pairs={{0,12},{1,13},{2,14},{3,15},{4,0},{5,1},{6,2},{7,3},{8,4},{9,5},{1... | collective-permute-start | bytes 1572872 | tf_op jit(solution)/shard_map/ppermute | solution.py:249
  46.2 12.7 %collective-permute-start.5 = (f32[2,256,256]{2,1,0:T(8,128)S(1)}, f32[2,256,256]{2,1,0:T(8,128)S(1)}, u32[]{:S(2)}, u32[]{:S(2)}) collective-permute-start(f32[2,256,256]{2,1,0:T(8,128)S(1)} %collective-permute-done.3.lower_left), channel_id=1, source_target_pairs={{1,0},{2,1},{3,2},{4,3},{5,4},{6,5},{7,6},{9,8},{10,9},{11,10},{12... | collective-permute-start | bytes 1572872 | tf_op jit(solution)/shard_map/ppermute | solution.py:249
  48.1 10.7 %collective-permute-start.7 = (f32[2,256,256]{2,1,0:T(8,128)}, f32[2,256,256]{2,1,0:T(8,128)S(1)}, u32[]{:S(2)}, u32[]{:S(2)}) collective-permute-start(f32[2,256,256]{2,1,0:T(8,128)} %collective-permute-done.6), channel_id=1, source_target_pairs={{4,7},{12,15},{20,23},{28,31},{36,39},{44,47},{52,55},{60,63},{68,... | collective-permute-start | bytes 1572872 | tf_op jit(solution)/shard_map/ppermute | solution.py:249
  58.9 1.0 copy-start.2
  78.4 7.6 %collective-permute-start.9 = (f32[2,512,256]{2,1,0:T(8,128)}, f32[2,512,256]{2,1,0:T(8,128)S(1)}, u32[]{:S(2)}, u32[]{:S(2)}) collective-permute-start(f32[2,512,256]{2,1,0:T(8,128)} %get-tuple-element.11), channel_id=1, source_target_pairs={{7,0},{15,8},{23,16},{31,24},{39,32},{47,40},{55,48},{63,56},{71,6... | collective-permute-start | bytes 3145736 | tf_op jit(solution)/shard_map/ppermute | solution.py:249
  79.1 35.9 %collective-permute-start.8 = (f32[2,512,256]{2,1,0:T(8,128)}, f32[2,512,256]{2,1,0:T(8,128)S(1)}, u32[]{:S(2)}, u32[]{:S(2)}) collective-permute-start(f32[2,512,256]{2,1,0:T(8,128)} %get-tuple-element.11), channel_id=1, source_target_pairs={{0,1},{1,2},{2,3},{3,4},{4,5},{5,6},{6,7},{8,9},{9,10},{10,11},{11... | collective-permute-start | bytes 3145736 | tf_op jit(solution)/shard_map/ppermute | solution.py:249
  85.9 28.8 %collective-permute-start.11 = (f32[2,256,256]{2,1,0:T(8,128)S(1)}, f32[2,256,256]{2,1,0:T(8,128)S(1)}, u32[]{:S(2)}, u32[]{:S(2)}) collective-permute-start(f32[2,256,256]{2,1,0:T(8,128)S(1)} %get-tuple-element.13), channel_id=1, source_target_pairs={{0,1},{1,2},{2,3},{3,4},{4,5},{5,6},{6,7},{7,8},{8,9},{9,10},{10,1... | collective-permute-start | bytes 1572872 | tf_op jit(solution)/shard_map/ppermute | solution.py:249
  86.0 29.0 %collective-permute-start.10 = (f32[2,512,256]{2,1,0:T(8,128)S(1)}, f32[2,512,256]{2,1,0:T(8,128)S(1)}, u32[]{:S(2)}, u32[]{:S(2)}) collective-permute-start(f32[2,512,256]{2,1,0:T(8,128)S(1)} %collective-permute-done.9), channel_id=1, source_target_pairs={{0,8},{8,0},{16,24},{24,16},{32,40},{40,32},{48,56},{56,48},{64,72... | collective-permute-start | bytes 3145736 | tf_op jit(solution)/shard_map/ppermute | solution.py:249
  86.7 56.7 %collective-permute-start.13 = (f32[2,256,256]{2,1,0:T(8,128)S(1)}, f32[2,256,256]{2,1,0:T(8,128)S(1)}, u32[]{:S(2)}, u32[]{:S(2)}) collective-permute-start(f32[2,256,256]{2,1,0:T(8,128)S(1)} %get-tuple-element.14), channel_id=1, source_target_pairs={{0,4},{1,5},{2,6},{3,7},{4,8},{5,9},{6,10},{7,11},{8,12},{9,13},{1... | collective-permute-start | bytes 1572872 | tf_op jit(solution)/shard_map/ppermute | solution.py:249
  114.7 34.1 %copy-start.3 = (f32[2,512,512]{2,1,0:T(8,128)S(1)}, f32[2,512,512]{2,1,0:T(8,128)}, u32[]{:S(2)}) copy-start(f32[2,512,512]{2,1,0:T(8,128)} %get-tuple-element.10) | copy-start | bytes 6291460
  114.8 34.1 %collective-permute-start.12 = (f32[2,256,256]{2,1,0:T(8,128)S(1)}, f32[2,256,256]{2,1,0:T(8,128)S(1)}, u32[]{:S(2)}, u32[]{:S(2)}) collective-permute-start(f32[2,256,256]{2,1,0:T(8,128)S(1)} %add.18), channel_id=1, source_target_pairs={{0,4},{1,5},{2,6},{3,7},{4,8},{5,9},{6,10},{7,11},{8,12},{9,13},{1... | collective-permute-start | bytes 1572872 | tf_op jit(solution)/shard_map/ppermute | solution.py:249
  150.7 4.3 %copy-start.5 = (f32[2,16,8]{1,2,0:T(8,128)S(1)}, f32[2,16,8]{1,2,0:T(8,128)}, u32[]{:S(2)}) copy-start(f32[2,16,8]{1,2,0:T(8,128)} %param.11) | copy-start | bytes 3076
  150.7 50.8 %all-to-all-start = ((f32[16,2,32,512]{3,2,1,0:T(8,128)}), f32[16,2,32,512]{3,2,1,0:T(8,128)S(1)}, u32[]{:S(2)}, u32[]{:S(2)}) async-start(f32[16,2,32,512]{3,2,1,0:T(8,128)} %bitcast.19), calls=%async_computation | async-start | bytes 4194304 | tf_op jit(solution)/shard_map/all_to_all | solution.py:280

commit v6 on v5

--- a/solution.py
+++ b/solution.py
@@ -267,6 +267,7 @@
     above_right = move(to_lower_right, [(t, t + TILE_COLS) for t in range(tiles)])
     left_step = move(to_right, [(last, 0), (half + last, half)])
     left = move(to_right, [(t, t + 1) for t in range(tiles) if t % half != last])
+    left_step, beside = lax.optimization_barrier((left_step, beside))
     left_far = move(left_step, [(0, half), (half, 0)])
     above_left = move(to_lower_left + beside, [(t, t + TILE_COLS) for t in range(tiles)])
     above = jnp.concatenate([above_left, above_right], 2)

time: 263 us -> 261 us (level)
  the two profiles are of different devices: /device:TPU:9 before, /device:TPU:136 now
where the time goes in v6:
time: 261 us; the launch traced here: 260 us
  waiting for transfers between devices  108 us (41%)
  starting transfers between devices  63.8 us (24%)
  blocking collectives  54.8 us (21%)
  Pallas kernels  24 us (9%)
  local copies, waits for them, and re-layouts  7.62 us (3%)
    ppermute x14, waiting for transfers between devices, move(): lax.ppermute(value, 'tile', [(s % tiles, d % tiles) for s, d in pairs])  58.8 us
    all_to_all x1, blocking collectives, body(): lax.all_to_all(spectra, 'energy', split_axis=0, concat_axis=0, tiled=True)  54.8 us
    all_to_all x1, waiting for transfers between devices, body(): lax.all_to_all(outgoing, 'energy', split_axis=0, concat_axis=0, tiled=True)  49.1 us
    ppermute x14, starting transfers between devices, move(): lax.ppermute(value, 'tile', [(s % tiles, d % tiles) for s, d in pairs])  35.8 us
    all_to_all x1, starting transfers between devices, body(): lax.all_to_all(outgoing, 'energy', split_axis=0, concat_axis=0, tiled=True)  28.1 us
    pallas_call x1, Pallas kernels, patch_gradients(): pl.pallas_call(gradient_kernel, out_shape=[f32((2, tile_px, tile_px)), f3...  18.4 us
    pallas_call x1, Pallas kernels, fit_spectra(): pl.pallas_call(fit_kernel, out_shape=jax.ShapeDtypeStruct(data.shape, jnp...  5.67 us
  transfers between devices with their start and end apart: 15, of which 7 were waited for; matrix products, arithmetic and copies ran while one was open for 1% of the time, Pallas kernels for 0%

profile of v6, /device:TPU:136, one launch (start us, length us, event | category | flops | bytes accessed | tf_op | source)
XLA Modules:
  0.0 260.4 jit_solution(11097714811129880367)
XLA Ops:
  0.0 2.4 slice.14
  2.4 1.7 collective-permute-start.1
  4.1 0.9 fusion.1
  5.0 0.5 collective-permute-start.3
  5.4 1.4 collective-permute-start.6
  6.9 2.4 collective-permute-start
  9.3 1.6 collective-permute-start.2
  11.0 0.7 collective-permute-start.4
  11.7 8.5 %collective-permute-done.3.lower_left = f32[2,256,256]{2,1,0:T(8,128)S(1)} collective-permute-done((f32[2,256,256]{2,1,0:T(8,128)S(1)}, f32[2,256,256]{2,1,0:T(8,128)S(1)}, u32[]{:S(2)}, u32[]{:S(2)}) %collective-permute-start.3) | collective-permute-done | bytes 524320 | tf_op jit(solution)/shard_map/ppermute | solution.py:249
  20.2 5.0 %collective-permute-start.5 = (f32[2,256,256]{2,1,0:T(8,128)S(1)}, f32[2,256,256]{2,1,0:T(8,128)S(1)}, u32[]{:S(2)}, u32[]{:S(2)}) collective-permute-start(f32[2,256,256]{2,1,0:T(8,128)S(1)} %collective-permute-done.3.lower_left), channel_id=1, source_target_pairs={{1,0},{2,1},{3,2},{4,3},{5,4},{6,5},{7,6},{9,8},{10,9},{11,10},{12... | collective-permute-start | bytes 1572872 | tf_op jit(solution)/shard_map/ppermute | solution.py:249
  25.3 0.7 collective-permute-start.7
  26.1 11.0 %collective-permute-done.4.lower_right = f32[2,256,256]{2,1,0:T(8,128)S(1)} collective-permute-done((f32[2,256,256]{2,1,0:T(8,128)}, f32[2,256,256]{2,1,0:T(8,128)S(1)}, u32[]{:S(2)}, u32[]{:S(2)}) %collective-permute-start.4) | collective-permute-done | bytes 524320 | tf_op jit(solution)/shard_map/ppermute | solution.py:249
  37.0 10.8 %collective-permute-done.5.corner = f32[2,256,256]{2,1,0:T(8,128)S(1)} collective-permute-done((f32[2,256,256]{2,1,0:T(8,128)S(1)}, f32[2,256,256]{2,1,0:T(8,128)S(1)}, u32[]{:S(2)}, u32[]{:S(2)}) %collective-permute-start.5) | collective-permute-done | bytes 524320 | tf_op jit(solution)/shard_map/ppermute | solution.py:249
  47.8 1.0 copy-done.2
  48.9 18.4 %patch_gradients.1 = (f32[2,512,512]{2,1,0:T(8,128)}, f32[2,512,256]{2,1,0:T(8,128)}, f32[2,256,256]{2,1,0:T(8,128)S(1)}, f32[2,256,256]{2,1,0:T(8,128)S(1)}, f32[2,256,256]{2,1,0:T(8,128)S(1)}) custom-call(s32[16,2]{1,0:T(8,128)S(1)} %copy.11.corners, f32[2,512,512]{2,1,0:T(8,128)} %bitcast.22, f32[2,512,256]{2,1,0:T(8,128)} %collective-permute-done.right, ...), custom_call_target="tpu_custom_call" | custom-call | flops 8589934592 | bytes 8388608 | tf_op jit(solution)/shard_map/patch_gradients/pallas_call | solution.py:161
  67.2 0.7 collective-permute-start.9
  68.0 7.2 %collective-permute-start.10 = (f32[2,256,256]{2,1,0:T(8,128)S(1)}, f32[2,256,256]{2,1,0:T(8,128)S(1)}, u32[]{:S(2)}, u32[]{:S(2)}) collective-permute-start(f32[2,256,256]{2,1,0:T(8,128)S(1)} %get-tuple-element.14), channel_id=1, source_target_pairs={{0,1},{1,2},{2,3},{3,4},{4,5},{5,6},{6,7},{7,8},{8,9},{9,10},{10,1... | collective-permute-start | bytes 1572872 | tf_op jit(solution)/shard_map/ppermute | solution.py:249
  75.2 7.6 %collective-permute-start.8 = (f32[2,512,256]{2,1,0:T(8,128)}, f32[2,512,256]{2,1,0:T(8,128)S(1)}, u32[]{:S(2)}, u32[]{:S(2)}) collective-permute-start(f32[2,512,256]{2,1,0:T(8,128)} %get-tuple-element.13), channel_id=1, source_target_pairs={{0,1},{1,2},{2,3},{3,4},{4,5},{5,6},{6,7},{8,9},{9,10},{10,11},{11... | collective-permute-start | bytes 3145736 | tf_op jit(solution)/shard_map/ppermute | solution.py:249
  82.9 0.7 collective-permute-start.11
  83.6 4.9 %collective-permute-start.13 = (f32[2,256,256]{2,1,0:T(8,128)S(1)}, f32[2,256,256]{2,1,0:T(8,128)S(1)}, u32[]{:S(2)}, u32[]{:S(2)}) collective-permute-start(f32[2,256,256]{2,1,0:T(8,128)S(1)} %get-tuple-element.18), channel_id=1, source_target_pairs={{0,4},{1,5},{2,6},{3,7},{4,8},{5,9},{6,10},{7,11},{8,12},{9,13},{1... | collective-permute-start | bytes 1572872 | tf_op jit(solution)/shard_map/ppermute | solution.py:249
  88.5 0.5 collective-permute-start.12
  89.1 2.4 collective-permute-done.8
  91.7 9.5 %collective-permute-done.13 = f32[2,256,256]{2,1,0:T(8,128)S(1)} collective-permute-done((f32[2,256,256]{2,1,0:T(8,128)S(1)}, f32[2,256,256]{2,1,0:T(8,128)S(1)}, u32[]{:S(2)}, u32[]{:S(2)}) %collective-permute-start.13) | collective-permute-done | bytes 524320 | tf_op jit(solution)/shard_map/ppermute | solution.py:249
  101.1 16.6 %collective-permute-done.12 = f32[2,256,256]{2,1,0:T(8,128)S(1)} collective-permute-done((f32[2,256,256]{2,1,0:T(8,128)S(1)}, f32[2,256,256]{2,1,0:T(8,128)S(1)}, u32[]{:S(2)}, u32[]{:S(2)}) %collective-permute-start.12) | collective-permute-done | bytes 524320 | tf_op jit(solution)/shard_map/ppermute | solution.py:249
  117.8 0.4 fusion
  118.1 1.5 copy.16
  119.6 28.1 %all-to-all-start = ((f32[16,2,32,512]{3,2,1,0:T(8,128)}), f32[16,2,32,512]{3,2,1,0:T(8,128)S(1)}, u32[]{:S(2)}, u32[]{:S(2)}) async-start(f32[16,2,32,512]{3,2,1,0:T(8,128)} %bitcast.19), calls=%async_computation | async-start | bytes 4194304 | tf_op jit(solution)/shard_map/all_to_all | solution.py:281
  147.9 0.8 select_reduce_fusion
  149.4 49.1 %all-to-all-done.data = f32[16,2,32,512]{3,2,1,0:T(8,128)S(1)} async-done(((f32[16,2,32,512]{3,2,1,0:T(8,128)}), f32[16,2,32,512]{3,2,1,0:T(8,128)S(1)}, u32[]{:S(2)}, u32[]{:S(2)}) %all-to-all-start) | async-done | bytes 2097184 | tf_op jit(solution)/shard_map/all_to_all | solution.py:281
  198.4 5.7 %fit_spectra.1 = f32[16,2,32,512]{3,2,1,0:T(8,128)S(1)} custom-call(f32[2,128]{1,0:T(2,128)S(1)} %reshape.12.spectra, f32[8,8]{1,0:T(8,128)S(1)} %multiply_subtract_fusion.step, f32[1]{0:T(128)} %bitcast.1.rate, f32[16,2,32,512]{3,2,1,0:T(8,128)S(1)} %all-to-all-done.data), custom_call_target="tpu_custom_call" | custom-call | tf_op jit(solution)/shard_map/fit_spectra/pallas_call | solution.py:230
  204.1 54.8 %all_to_all.10 = f32[16,2,32,512]{3,2,1,0:T(8,128)S(1)} all-to-all(f32[16,2,32,512]{3,2,1,0:T(8,128)S(1)} %fit_spectra.1), channel_id=1, replica_groups=mesh['energy'=16,'tile'=16] {'energy'}, dimensions={0} | all-to-all | bytes 4194304 | tf_op jit(solution)/shard_map/all_to_all | solution.py:283
  258.9 1.5 copy.13
  (27 shorter events, 0.5 us)
Async XLA Ops:
  0.0 4.1 %copy-start.4 = (f32[1,2,1,512,512]{4,3,2,1,0:T(8,128)S(1)}, f32[1,2,1,512,512]{4,3,2,1,0:T(8,128)}, u32[]{:S(2)}) copy-start(f32[1,2,1,512,512]{4,3,2,1,0:T(8,128)} %param.7) | copy-start | bytes 6291460
  0.0 26.0 %copy-start.6 = (s32[1,16,2]{1,2,0:T(2,128)S(1)}, s32[1,16,2]{1,2,0:T(2,128)}, u32[]{:S(2)}) copy-start(s32[1,16,2]{1,2,0:T(2,128)} %param.10) | copy-start | bytes 388
  0.0 47.8 %copy-start = (f32[1,2,256,256]{3,2,1,0:T(8,128)S(1)}, f32[1,2,256,256]{3,2,1,0:T(8,128)}, u32[]{:S(2)}) copy-start(f32[1,2,256,256]{3,2,1,0:T(8,128)} %param.8) | copy-start | bytes 1572868
  0.0 47.8 %copy-start.1 = (bf16[512,512]{1,0:T(8,128)(2,1)S(1)}, bf16[512,512]{1,0:T(8,128)(2,1)}, u32[]{:S(2)}) copy-start(bf16[512,512]{1,0:T(8,128)(2,1)} %constant.13.clone.left_table) | copy-start | bytes 1572868
  2.4 6.9 %collective-permute-start.1 = (f32[2,512,256]{2,1,0:T(8,128)}, f32[2,512,256]{2,1,0:T(8,128)}, u32[]{:S(2)}, u32[]{:S(2)}) collective-permute-start(f32[2,512,256]{2,1,0:T(8,128)} %slice.14), channel_id=1, source_target_pairs={{0,7},{8,15},{16,23},{24,31},{32,39},{40,47},{48,55},{56,63},{64,7... | collective-permute-start | bytes 3145736 | tf_op jit(solution)/shard_map/ppermute | solution.py:249
  5.0 15.3 %collective-permute-start.3 = (f32[2,256,256]{2,1,0:T(8,128)S(1)}, f32[2,256,256]{2,1,0:T(8,128)S(1)}, u32[]{:S(2)}, u32[]{:S(2)}) collective-permute-start(f32[2,256,256]{2,1,0:T(8,128)S(1)} %get-tuple-element.20), channel_id=1, source_target_pairs={{0,12},{1,13},{2,14},{3,15},{4,0},{5,1},{6,2},{7,3},{8,4},{9,5},{1... | collective-permute-start | bytes 1572872 | tf_op jit(solution)/shard_map/ppermute | solution.py:249
  5.4 19.8 %collective-permute-start.6 = (f32[2,256,256]{2,1,0:T(8,128)S(1)}, f32[2,256,256]{2,1,0:T(8,128)}, u32[]{:S(2)}, u32[]{:S(2)}) collective-permute-start(f32[2,256,256]{2,1,0:T(8,128)S(1)} %get-tuple-element.20), channel_id=1, source_target_pairs={{4,12},{12,4},{20,28},{28,20},{36,44},{44,36},{52,60},{60,52},{68,... | collective-permute-start | bytes 1572872 | tf_op jit(solution)/shard_map/ppermute | solution.py:249
  6.9 40.9 %collective-permute-start = (f32[2,512,256]{2,1,0:T(8,128)}, f32[2,512,256]{2,1,0:T(8,128)}, u32[]{:S(2)}, u32[]{:S(2)}) collective-permute-start(f32[2,512,256]{2,1,0:T(8,128)} %slice.14), channel_id=1, source_target_pairs={{1,0},{2,1},{3,2},{4,3},{5,4},{6,5},{7,6},{9,8},{10,9},{11,10},{12... | collective-permute-start | bytes 3145736 | tf_op jit(solution)/shard_map/ppermute | solution.py:249
  9.3 38.5 %collective-permute-start.2 = (f32[2,512,256]{2,1,0:T(8,128)}, f32[2,512,256]{2,1,0:T(8,128)}, u32[]{:S(2)}, u32[]{:S(2)}) collective-permute-start(f32[2,512,256]{2,1,0:T(8,128)} %collective-permute-done.1), channel_id=1, source_target_pairs={{7,15},{15,7},{23,31},{31,23},{39,47},{47,39},{55,63},{63,55},{71,... | collective-permute-start | bytes 3145736 | tf_op jit(solution)/shard_map/ppermute | solution.py:249
  11.0 26.1 %collective-permute-start.4 = (f32[2,256,256]{2,1,0:T(8,128)}, f32[2,256,256]{2,1,0:T(8,128)S(1)}, u32[]{:S(2)}, u32[]{:S(2)}) collective-permute-start(f32[2,256,256]{2,1,0:T(8,128)} %get-tuple-element.19), channel_id=1, source_target_pairs={{0,12},{1,13},{2,14},{3,15},{4,0},{5,1},{6,2},{7,3},{8,4},{9,5},{1... | collective-permute-start | bytes 1572872 | tf_op jit(solution)/shard_map/ppermute | solution.py:249
  20.2 27.6 %collective-permute-start.5 = (f32[2,256,256]{2,1,0:T(8,128)S(1)}, f32[2,256,256]{2,1,0:T(8,128)S(1)}, u32[]{:S(2)}, u32[]{:S(2)}) collective-permute-start(f32[2,256,256]{2,1,0:T(8,128)S(1)} %collective-permute-done.3.lower_left), channel_id=1, source_target_pairs={{1,0},{2,1},{3,2},{4,3},{5,4},{6,5},{7,6},{9,8},{10,9},{11,10},{12... | collective-permute-start | bytes 1572872 | tf_op jit(solution)/shard_map/ppermute | solution.py:249
  25.3 22.5 %collective-permute-start.7 = (f32[2,256,256]{2,1,0:T(8,128)}, f32[2,256,256]{2,1,0:T(8,128)S(1)}, u32[]{:S(2)}, u32[]{:S(2)}) collective-permute-start(f32[2,256,256]{2,1,0:T(8,128)} %collective-permute-done.6), channel_id=1, source_target_pairs={{4,7},{12,15},{20,23},{28,31},{36,39},{44,47},{52,55},{60,63},{68,... | collective-permute-start | bytes 1572872 | tf_op jit(solution)/shard_map/ppermute | solution.py:249
  47.8 1.0 copy-start.2
  67.2 15.6 %collective-permute-start.9 = (f32[2,512,256]{2,1,0:T(8,128)}, f32[2,512,256]{2,1,0:T(8,128)S(1)}, u32[]{:S(2)}, u32[]{:S(2)}) collective-permute-start(f32[2,512,256]{2,1,0:T(8,128)} %get-tuple-element.13), channel_id=1, source_target_pairs={{7,0},{15,8},{23,16},{31,24},{39,32},{47,40},{55,48},{63,56},{71,6... | collective-permute-start | bytes 3145736 | tf_op jit(solution)/shard_map/ppermute | solution.py:249
  68.0 14.9 %collective-permute-start.10 = (f32[2,256,256]{2,1,0:T(8,128)S(1)}, f32[2,256,256]{2,1,0:T(8,128)S(1)}, u32[]{:S(2)}, u32[]{:S(2)}) collective-permute-start(f32[2,256,256]{2,1,0:T(8,128)S(1)} %get-tuple-element.14), channel_id=1, source_target_pairs={{0,1},{1,2},{2,3},{3,4},{4,5},{5,6},{6,7},{7,8},{8,9},{9,10},{10,1... | collective-permute-start | bytes 1572872 | tf_op jit(solution)/shard_map/ppermute | solution.py:249
  75.2 16.3 %collective-permute-start.8 = (f32[2,512,256]{2,1,0:T(8,128)}, f32[2,512,256]{2,1,0:T(8,128)S(1)}, u32[]{:S(2)}, u32[]{:S(2)}) collective-permute-start(f32[2,512,256]{2,1,0:T(8,128)} %get-tuple-element.13), channel_id=1, source_target_pairs={{0,1},{1,2},{2,3},{3,4},{4,5},{5,6},{6,7},{8,9},{9,10},{10,11},{11... | collective-permute-start | bytes 3145736 | tf_op jit(solution)/shard_map/ppermute | solution.py:249
  82.9 8.7 %collective-permute-start.11 = (f32[2,512,256]{2,1,0:T(8,128)S(1)}, f32[2,512,256]{2,1,0:T(8,128)S(1)}, u32[]{:S(2)}, u32[]{:S(2)}) collective-permute-start(f32[2,512,256]{2,1,0:T(8,128)S(1)} %collective-permute-done.9), channel_id=1, source_target_pairs={{0,8},{8,0},{16,24},{24,16},{32,40},{40,32},{48,56},{56,48},{64,72... | collective-permute-start | bytes 3145736 | tf_op jit(solution)/shard_map/ppermute | solution.py:249
  83.6 17.5 %collective-permute-start.13 = (f32[2,256,256]{2,1,0:T(8,128)S(1)}, f32[2,256,256]{2,1,0:T(8,128)S(1)}, u32[]{:S(2)}, u32[]{:S(2)}) collective-permute-start(f32[2,256,256]{2,1,0:T(8,128)S(1)} %get-tuple-element.18), channel_id=1, source_target_pairs={{0,4},{1,5},{2,6},{3,7},{4,8},{5,9},{6,10},{7,11},{8,12},{9,13},{1... | collective-permute-start | bytes 1572872 | tf_op jit(solution)/shard_map/ppermute | solution.py:249
  88.5 29.3 %copy-start.3 = (f32[2,512,512]{2,1,0:T(8,128)S(1)}, f32[2,512,512]{2,1,0:T(8,128)}, u32[]{:S(2)}) copy-start(f32[2,512,512]{2,1,0:T(8,128)} %get-tuple-element.12) | copy-start | bytes 6291460
  88.5 29.2 %collective-permute-start.12 = (f32[2,256,256]{2,1,0:T(8,128)S(1)}, f32[2,256,256]{2,1,0:T(8,128)S(1)}, u32[]{:S(2)}, u32[]{:S(2)}) collective-permute-start(f32[2,256,256]{2,1,0:T(8,128)S(1)} %add.18), channel_id=1, source_target_pairs={{0,4},{1,5},{2,6},{3,7},{4,8},{5,9},{6,10},{7,11},{8,12},{9,13},{1... | collective-permute-start | bytes 1572872 | tf_op jit(solution)/shard_map/ppermute | solution.py:249
  119.6 28.1 %copy-start.5 = (f32[2,16,8]{1,2,0:T(8,128)S(1)}, f32[2,16,8]{1,2,0:T(8,128)}, u32[]{:S(2)}) copy-start(f32[2,16,8]{1,2,0:T(8,128)} %param.11) | copy-start | bytes 3076
  119.6 78.8 %all-to-all-start = ((f32[16,2,32,512]{3,2,1,0:T(8,128)}), f32[16,2,32,512]{3,2,1,0:T(8,128)S(1)}, u32[]{:S(2)}, u32[]{:S(2)}) async-start(f32[16,2,32,512]{3,2,1,0:T(8,128)} %bitcast.19), calls=%async_computation | async-start | bytes 4194304 | tf_op jit(solution)/shard_map/all_to_all | solution.py:281
